TPU v7x, 32 devices: a whole 2x2x4 slice. The times are simulated.
32 devices in a mesh: mode: 4 (over x, core), batch: 4 (over z), cores: 2 (over y).
Axes of the slice: x: 2, y: 2, z: 4, core: 2. Of those that a mesh axis runs over, the one named last changes fastest.
Arguments:
- fields: bfloat16 [4, 20, 1024, 1024], P('batch', None, ('mode', 'cores')), may hold values from -6 to 6
- lift_weight: bfloat16 [20, 128], replicated, may hold values from -1.25 to 1.25
- lift_bias: float32 [128], replicated, may hold values from -3 to 3
- first_core: bfloat16 [128, 32, 32], P('batch'), may hold values from -1 to 1
- second_core: bfloat16 [128, 32, 32], P(('mode', 'cores')), may hold values from -1 to 1
- input_core: bfloat16 [128, 32, 32], P('batch'), may hold values from -0.09375 to 0.09375
- output_core: bfloat16 [128, 2, 32, 32], P('batch'), may hold values from -3 to 3
- skip_weight: bfloat16 [128, 128], replicated, may hold values from -0.5 to 0.5
- skip_bias: float32 [128], replicated, may hold values from -3 to 3
- out_weight: bfloat16 [128, 20], replicated, may hold values from -0.5 to 0.5
- out_bias: float32 [20], replicated, may hold values from -3 to 3
Outputs:
- updated: bfloat16 [4, 20, 1024, 1024], P('batch', None, ('mode', 'cores'))
All inputs are finite; a program needn't handle non-finite values.
Results may differ from a plain program's by a relative error of at most 0.012.
Values may be sent and summed in bfloat16 or wider, within the bound.
A program may use at most 256 MiB of HBM per device.

v0:
```python
import functools
import math

import jax
import jax.numpy as jnp
import ml_dtypes
import numpy as np
from jax import lax
from jax.experimental import pallas as pl
from jax.experimental.pallas import tpu as pltpu
from jax.sharding import PartitionSpec as P

NX = 1024
NY = 1024
MX = 128
MY = 128


TWO_PI = 2.0 * math.pi


def wave_pair(waves, points, length):
    phase_step = waves[:, None] * points[None, :] % length
    angles = phase_step.astype(jnp.float32) * (TWO_PI / length)
    return (jnp.cos(angles), jnp.sin(angles))


def width_forward(length, wave_count):
    points = jnp.arange(length, dtype=jnp.int32)
    waves = jnp.arange(wave_count, dtype=jnp.int32)
    cosines, sine_part = wave_pair(points, waves, length)
    stacked = jnp.stack([cosines, -sine_part], axis=1) / math.sqrt(length)
    return stacked.astype(jnp.bfloat16)


def height_forward(row_index, wave_count, length):
    waves = jnp.arange(wave_count, dtype=jnp.int32) - wave_count // 2
    cosines, sine_part = wave_pair(waves, row_index, length)
    upper = jnp.stack([cosines, sine_part], axis=1)
    lower = jnp.stack([-sine_part, cosines], axis=1)
    return (jnp.stack([upper, lower], axis=0) / math.sqrt(length)).astype(jnp.bfloat16)


def height_inverse(row_index, wave_count, length):
    waves = jnp.arange(wave_count, dtype=jnp.int32) - wave_count // 2
    cosines, sine_part = wave_pair(row_index, waves, length)
    upper = jnp.stack([cosines, -sine_part], axis=1)
    lower = jnp.stack([sine_part, cosines], axis=1)
    return (jnp.stack([upper, lower], axis=0) / math.sqrt(length)).astype(jnp.bfloat16)


def width_inverse(waves, length):
    points = jnp.arange(length, dtype=jnp.int32)
    cosines, sine_part = wave_pair(waves, points, length)
    weight = jnp.where(waves == 0, 1.0, 2.0).astype(jnp.float32)[:, None]
    stacked = jnp.stack([cosines * weight, -sine_part * weight], axis=0) / math.sqrt(length)
    return stacked.astype(jnp.bfloat16)


def bias_modes(lift_bias, wave_index, length):
    real_row = (
        jnp.where(wave_index == 0, 1.0, 0.0).astype(jnp.float32)[:, None]
        * (math.sqrt(length) * lift_bias)[None, :]
    )
    return jnp.stack([real_row, jnp.zeros_like(real_row)], axis=0)


def lift_modes(modes, lift_weight, lift_bias, wave_index):
    lifted_modes = jnp.einsum(
        "fabpmv,vc->fabpmc", modes, lift_weight, preferred_element_type=jnp.float32
    )
    return (lifted_modes + bias_modes(lift_bias, wave_index, NY)).astype(jnp.bfloat16)


def grid_rows(stored, row_count, holder_count):
    return stored % row_count * holder_count + stored // row_count


def shards(
    fields,
    lift_weight,
    lift_bias,
    first_core,
    second_core,
    input_core,
    output_core,
    skip_weight,
    skip_bias,
    out_weight,
    out_bias,
):
    mode_count = lax.axis_size("mode")
    core_count = lax.axis_size("cores")
    row_count = fields.shape[2]
    block_size = second_core.shape[0]
    block_start = (lax.axis_index("mode") * core_count + lax.axis_index("cores")) * block_size
    local_waves = block_start + jnp.arange(block_size, dtype=jnp.int32)
    lifted = (
        jnp.einsum("fvxy,vc->fxyc", fields, lift_weight, preferred_element_type=jnp.float32)
        + lift_bias
    ).astype(jnp.bfloat16)
    field_modes = jnp.einsum(
        "fvxy,ypk->fxpkv", fields, width_forward(NY, MY), preferred_element_type=jnp.float32
    ).astype(jnp.bfloat16)
    field_modes = field_modes[:, None]
    gathered = (
        lax.all_gather(first_core, "batch", axis=0, tiled=True),
        lax.all_gather(input_core, "batch", axis=0, tiled=True),
        lax.all_gather(output_core, "batch", axis=0, tiled=True),
    )
    first_whole, input_whole, output_whole = gathered
    mode_factor = jnp.einsum(
        "kab,mbd->kmad", first_whole, second_core, preferred_element_type=jnp.float32
    ).astype(jnp.bfloat16)
    arrived = lax.all_to_all(
        field_modes, ("mode", "cores"), split_axis=4, concat_axis=2, tiled=True
    )
    rows_held = jnp.arange(NX, dtype=jnp.int32)[None, :]
    by_mode = lift_modes(arrived, lift_weight, lift_bias, local_waves)
    lead_rows = rows_held.shape[0]
    side_rows = rows_held.shape[1]
    flat_rows = grid_rows(rows_held.reshape(-1), row_count, mode_count * core_count)
    height_table = height_forward(flat_rows, MX, NX).reshape(2, MX, 2, lead_rows, side_rows)
    spectrum = jnp.einsum(
        "qkpab,fabpmc->fqkmc", height_table, by_mode, preferred_element_type=jnp.float32
    ).astype(jnp.bfloat16)
    projected = jnp.einsum(
        "fqkmc,cbe->fqkmbe", spectrum, input_whole, preferred_element_type=jnp.float32
    ).astype(jnp.bfloat16)
    carried = jnp.einsum(
        "kmab,fqkmbe->fqkmae", mode_factor, projected, preferred_element_type=jnp.float32
    ).astype(jnp.bfloat16)
    traced = jnp.einsum(
        "fqkmae,osea->fqkmso", carried, output_whole, preferred_element_type=jnp.float32
    )
    real_part = traced[:, 0, :, :, 0, :] - traced[:, 1, :, :, 1, :]
    imaginary = traced[:, 0, :, :, 1, :] + traced[:, 1, :, :, 0, :]
    mixed_modes = jnp.stack([real_part, imaginary], axis=1).astype(jnp.bfloat16)
    height_back = height_inverse(flat_rows, MX, NX).reshape(2, lead_rows, side_rows, 2, MX)
    col_modes = jnp.einsum(
        "pabqk,fqkmc->fabpmc", height_back, mixed_modes, preferred_element_type=jnp.float32
    ).astype(jnp.bfloat16)
    returned = lax.all_to_all(col_modes, ("mode", "cores"), split_axis=2, concat_axis=4, tiled=True)
    waves_held = jnp.arange(MY, dtype=jnp.int32)
    width_back = width_inverse(waves_held, NY)
    spatial = jnp.einsum(
        "fxpmc,pmy->fxyc", returned[:, 0], width_back, preferred_element_type=jnp.float32
    )
    skip_term = jnp.einsum("fxyc,cd->fxyd", lifted, skip_weight, preferred_element_type=jnp.float32)
    active = jax.nn.gelu(spatial + skip_term + skip_bias, approximate=False).astype(jnp.bfloat16)
    result = (
        jnp.einsum("fxyc,cv->fvxy", active, out_weight, preferred_element_type=jnp.float32)
        + out_bias[:, None, None]
    )
    return result.astype(jnp.bfloat16)


def cyclic_rows(row_count, holders):
    return (np.arange(row_count)[None, :] * holders + np.arange(holders)[:, None]).reshape(-1)


def host_pair(waves, points, length):
    steps = np.asarray(waves)[:, None] * np.asarray(points)[None, :] % length
    angles = steps.astype(np.float32) * np.float32(TWO_PI / length)
    return np.cos(angles), np.sin(angles)


def dense(a, b, contract=((1,), (0,))):
    return lax.dot_general(a, b, (contract, ((), ())), preferred_element_type=jnp.float32)


GROUP = 4
PACK = 16


def mix_kernel(
    base, arrived, height, lift, row_sum, bias_row, joined, first, back, spread,
    mixed, stacked, spectrum, blocks, closing, weights, parts, carried,
):
    group = pl.program_id(0)
    holders, lead, _ = arrived.shape
    waves = lead // 2
    rank = first.shape[1]
    variables = stacked.shape[0] // waves
    row_count = arrived.shape[2] // variables
    kx_count = mixed.shape[0] // 2
    channels = joined.shape[1]
    packs = kx_count // PACK
    groups = spectrum.shape[0]
    span = rank * PACK
    wide = GROUP * rank

    @pl.when(group == 0)
    def _():
        for d in range(holders):
            for p in range(2):
                for v in range(variables):
                    stacked[v * waves:(v + 1) * waves, (d * 2 + p) * row_count:(d * 2 + p + 1) * row_count] = (
                        arrived[d, p * waves:(p + 1) * waves, v * row_count:(v + 1) * row_count]
                    )
        by_variable = dense(height[...], stacked[...], ((1,), (1,))).astype(jnp.bfloat16)
        for g in range(groups):
            lanes = slice((base + g) * GROUP * channels, (base + g + 1) * GROUP * channels)
            spectrum[g] = (
                dense(by_variable, lift[:, lanes]) + row_sum[...] * bias_row[:, lanes]
            ).astype(jnp.bfloat16)
        down = lax.broadcasted_iota(jnp.int32, (span, span), 0) % PACK
        across = lax.broadcasted_iota(jnp.int32, (span, span), 1) % PACK
        same = down == across
        for k in range(packs):
            full = dense(first[k * span:(k + 1) * span, :], spread[...])
            blocks[k] = jnp.where(same, full, 0.0).astype(jnp.bfloat16)
        closing[...] = jnp.zeros_like(closing)
        outs = back.shape[1]
        for a in range(rank):
            for m in range(GROUP):
                closing[(a * GROUP + m) * rank:(a * GROUP + m + 1) * rank, m * outs:(m + 1) * outs] = (
                    back[a * rank:(a + 1) * rank, :]
                )

    own = spectrum[group]
    owner = lax.broadcasted_iota(jnp.int32, (channels, wide), 1) // rank
    for part in range(rank // 8):
        for b in range(8):
            block = joined[part * 8 + b]
            for m in range(GROUP):
                weights[m * channels:(m + 1) * channels, b * wide:(b + 1) * wide] = jnp.where(
                    owner == m, block, jnp.zeros_like(block)
                )
        got = dense(own, weights[...]).astype(jnp.bfloat16)
        for b in range(8):
            for q in range(2):
                parts[part * 8 + b, :, q * wide:(q + 1) * wide] = got[
                    q * kx_count:(q + 1) * kx_count, b * wide:(b + 1) * wide
                ]
    for k in range(packs):
        rows = parts[:, k * PACK:(k + 1) * PACK, :].reshape(span, 2 * wide)
        got = dense(blocks[k], rows).astype(jnp.bfloat16)
        for a in range(rank):
            for q in range(2):
                carried[q * kx_count + k * PACK:q * kx_count + (k + 1) * PACK, a * wide:(a + 1) * wide] = got[
                    a * PACK:(a + 1) * PACK, q * wide:(q + 1) * wide
                ]
    traced = dense(carried[...], closing[...])
    outs = back.shape[1]
    for m in range(GROUP):
        one = traced[:, m * outs:(m + 1) * outs]
        real = one[:kx_count, :channels] - one[kx_count:, channels:]
        imaginary = one[:kx_count, channels:] + one[kx_count:, :channels]
        mixed[:kx_count, m * channels:(m + 1) * channels] = real.astype(jnp.bfloat16)
        mixed[kx_count:, m * channels:(m + 1) * channels] = imaginary.astype(jnp.bfloat16)


def mix(base, groups, arrived, height, lift, row_sum, bias_row, joined, first, back, spread):
    holders, lead, flat = arrived.shape
    waves = lead // 2
    variables = lift.shape[0] // waves
    rank, channels, _ = joined.shape
    kx2 = height.shape[0]
    kx_count = kx2 // 2
    span = rank * PACK
    wide = GROUP * rank

    def whole(a):
        return pl.BlockSpec(a.shape, lambda g: (0,) * a.ndim)

    return pl.pallas_call(
        functools.partial(mix_kernel, base),
        grid=(groups,),
        in_specs=[
            whole(arrived), whole(height), whole(lift), whole(row_sum), whole(bias_row),
            pl.BlockSpec((rank, channels, wide), lambda g: (0, 0, base + g)),
            whole(first), whole(back), whole(spread),
        ],
        out_specs=pl.BlockSpec((kx2, GROUP * channels), lambda g: (0, g)),
        out_shape=jax.ShapeDtypeStruct((kx2, groups * GROUP * channels), jnp.bfloat16),
        scratch_shapes=[
            pltpu.VMEM((variables * waves, height.shape[1]), jnp.bfloat16),
            pltpu.VMEM((groups, kx2, GROUP * channels), jnp.bfloat16),
            pltpu.VMEM((kx_count // PACK, span, span), jnp.bfloat16),
            pltpu.VMEM((rank * wide, GROUP * back.shape[1]), jnp.bfloat16),
            pltpu.VMEM((GROUP * channels, 8 * wide), jnp.bfloat16),
            pltpu.VMEM((rank, kx_count, 2 * wide), jnp.bfloat16),
            pltpu.VMEM((kx2, rank * wide), jnp.bfloat16),
        ],
        compiler_params=pltpu.CompilerParams(vmem_limit_bytes=48 * 2**20),
        cost_estimate=pl.CostEstimate(
            flops=groups * 7 * 10**9, bytes_accessed=8 * 2**20, transcendentals=0
        ),
        name="mix",
    )(arrived, height, lift, row_sum, bias_row, joined, first, back, spread)


def rows_kernel(table, gathered, *rest):
    cols, turned = rest[-2:]
    row_count, waves, channels = turned.shape
    for p in range(2):
        got = dense(table[p * row_count:(p + 1) * row_count, :], gathered[0])
        for m in range(waves):
            turned[:, m, :] = got[:, m * channels:(m + 1) * channels]
        cols[:, p] = turned[...].astype(jnp.bfloat16)


def rows_back(table, gathered, channels, half, halves, earlier):
    holders, kx2, flat = gathered.shape
    row_count = table.shape[0] // 2
    waves = flat // channels
    shape = (row_count, 2, holders * halves * waves, channels)
    extra = [] if earlier is None else [earlier]
    return pl.pallas_call(
        rows_kernel,
        grid=(holders,),
        in_specs=[
            pl.BlockSpec(table.shape, lambda d: (0, 0)),
            pl.BlockSpec((1, kx2, flat), lambda d: (d, 0, 0)),
        ] + [pl.BlockSpec(memory_space=pl.ANY) for _ in extra],
        input_output_aliases={2: 0} if extra else {},
        cost_estimate=pl.CostEstimate(
            flops=2 * holders * kx2 * kx2 * flat, bytes_accessed=16 * 2**20, transcendentals=0
        ),
        out_specs=pl.BlockSpec((row_count, 2, waves, channels), lambda d: (0, 0, d * halves + half, 0)),
        out_shape=jax.ShapeDtypeStruct(shape, jnp.bfloat16),
        scratch_shapes=[pltpu.VMEM((row_count, waves, channels), jnp.float32)],
        compiler_params=pltpu.CompilerParams(vmem_limit_bytes=48 * 2**20),
        name="rows_back",
    )(table, gathered, *extra)


LANES = 512
HALF = PACK // 2


def gelu(h):
    return h * (0.5 + 0.5 * lax.erf(h * (1.0 / math.sqrt(2.0))))


def finish_kernel(fields, cols, width, skip, bias, closing, out_bias, result, turned, source, active):
    variables, rows, points = fields.shape
    channels = cols.shape[2]
    for x in range(rows):
        turned[x * channels:(x + 1) * channels, :] = cols[x].T
    for h in range(2):
        source[h] = fields[:, h * HALF:(h + 1) * HALF, :].reshape(variables * HALF, points)

    def step(i, carry):
        start = pl.multiple_of(i * LANES, LANES)
        lanes = pl.ds(start, LANES)
        table = width[:, lanes]
        depth = 2 * channels
        for h in range(2):
            near = source[h, :, lanes]
            for x in range(HALF // 2):
                here = slice(x * depth, (x + 1) * depth)
                top = h * HALF * channels + x * depth
                total = dense(turned[top:top + depth, :], table) + dense(skip[here, :], near) + bias[here, :]
                active[here, :] = gelu(total).astype(jnp.bfloat16)
            got = dense(closing[...], active[...]) + out_bias[...]
            result[:, h * HALF:(h + 1) * HALF, lanes] = got.reshape(variables, HALF, LANES).astype(jnp.bfloat16)
        return carry

    lax.fori_loop(0, points // LANES, step, 0)


def finish(fields, cols, width, skip, bias, closing, out_bias):
    variables, row_count, points = fields.shape
    depth, channels = cols.shape[1:]

    def whole(a):
        return pl.BlockSpec(a.shape, lambda i: (0,) * a.ndim)

    return pl.pallas_call(
        finish_kernel,
        grid=(row_count // PACK,),
        in_specs=[
            pl.BlockSpec((variables, PACK, points), lambda i: (0, i, 0)),
            pl.BlockSpec((PACK, depth, channels), lambda i: (i, 0, 0)),
            whole(width), whole(skip), whole(bias), whole(closing), whole(out_bias),
        ],
        out_specs=pl.BlockSpec((variables, PACK, points), lambda i: (0, i, 0)),
        out_shape=jax.ShapeDtypeStruct(fields.shape, jnp.bfloat16),
        scratch_shapes=[
            pltpu.VMEM((PACK * channels, depth), jnp.bfloat16),
            pltpu.VMEM((2, variables * HALF, points), jnp.bfloat16),
            pltpu.VMEM((HALF * channels, LANES), jnp.bfloat16),
        ],
        compiler_params=pltpu.CompilerParams(vmem_limit_bytes=48 * 2**20),
        name="finish",
    )(fields, cols, width, skip, bias, closing, out_bias)


def gather_factors(first_core, input_core, output_core):
    count, rank, _ = first_core.shape
    first_core = first_core.reshape(count // PACK, PACK, rank, rank).transpose(0, 2, 1, 3)
    flat = jnp.concatenate(
        [first_core.reshape(-1), input_core.reshape(-1), output_core.reshape(-1)]
    ).reshape(-1, 128)
    whole = lax.all_gather(flat, "batch", axis=0, tiled=False)
    parts = whole.shape[0]
    size = first_core.size
    whole = whole.reshape(parts, -1)
    first = whole[:, :size].reshape(-1, rank)
    inner = whole[:, size:2 * size].reshape(parts * count, rank, rank)
    outer = whole[:, 2 * size:].reshape(parts * count, 2, rank, rank)
    return first, inner, outer


def fast_shards(
    fields, lift_weight, lift_bias, first_core, second_core, input_core, output_core,
    skip_weight, skip_bias, out_weight, out_bias,
):
    holders = lax.axis_size("mode") * lax.axis_size("cores")
    waves, rank, _ = second_core.shape
    _, variables, row_count, points = fields.shape
    channels = lift_weight.shape[1]
    fields = fields[0]
    me = lax.axis_index("mode") * lax.axis_size("cores") + lax.axis_index("cores")

    cosines, sines = host_pair(np.arange(MY), np.arange(points), points)
    root = math.sqrt(points)
    forward = np.stack([cosines, -sines], 0).reshape(2, holders, waves, points).transpose(1, 0, 2, 3)
    forward = jnp.asarray((forward.reshape(2 * MY, points) / root).astype(np.float32)).astype(jnp.bfloat16)
    weight = np.where(np.arange(MY) == 0, 1.0, 2.0).astype(np.float32)[:, None]
    width = np.concatenate([cosines * weight, -sines * weight], 0) / root
    width = jnp.asarray(width.astype(ml_dtypes.bfloat16))
    order = cyclic_rows(row_count, holders)
    root = math.sqrt(NX)
    cosines, sines = host_pair(np.arange(MX) - MX // 2, order, NX)
    cosines, sines = [t.reshape(MX, holders, row_count) / root for t in (cosines, sines)]
    upper = np.stack([cosines, sines], 2)
    lower = np.stack([-sines, cosines], 2)
    height = np.stack([upper, lower], 0).reshape(2 * MX, -1).astype(ml_dtypes.bfloat16)
    real_part = np.asarray(height, np.float32).reshape(2 * MX, holders, 2, row_count)[:, :, 0]
    row_sum = real_part.sum((1, 2), dtype=np.float64).astype(np.float32)[:, None]
    cos_t, sin_t = [t.transpose(1, 2, 0) for t in (cosines, sines)]
    up = np.concatenate([cos_t, -sin_t], 2)
    low = np.concatenate([sin_t, cos_t], 2)
    back_rows = jnp.asarray(np.concatenate([up, low], 1).astype(ml_dtypes.bfloat16))
    back_rows = lax.dynamic_index_in_dim(back_rows, me, 0, keepdims=False)

    first, inner, outer = gather_factors(first_core, input_core, output_core)
    modes = jnp.einsum(
        "ry,vxy->rvx", forward, fields, preferred_element_type=jnp.float32
    ).astype(jnp.bfloat16)
    modes = modes.reshape(holders, 2 * waves, variables * row_count)
    arrived = lax.all_to_all(modes, ("mode", "cores"), split_axis=0, concat_axis=0, tiled=True)

    same = jnp.eye(waves, dtype=jnp.bfloat16)
    lift = (lift_weight[:, None, None, :] * same[None, :, :, None]).reshape(
        variables * waves, waves * channels
    )
    is_zero = (me * waves + jnp.arange(waves) == 0).astype(jnp.float32)
    bias_value = (math.sqrt(points) * lift_bias).astype(jnp.bfloat16).astype(jnp.float32)
    bias_row = (is_zero[:, None] * bias_value[None, :]).reshape(1, -1)
    joined = jnp.einsum(
        "mbd,cde->bcme", second_core, inner, preferred_element_type=jnp.float32
    ).astype(jnp.bfloat16).reshape(rank, channels, waves * rank)
    back = outer.transpose(3, 2, 1, 0).reshape(rank * rank, -1)
    spread = jnp.asarray(np.repeat(np.eye(rank), PACK, axis=1).astype(ml_dtypes.bfloat16))
    halves = 2
    groups = waves // GROUP // halves
    row_sum = jnp.asarray(row_sum)
    height = jnp.asarray(height)
    mixed = [
        mix(h * groups, groups, arrived, height, lift, row_sum, bias_row, joined, first, back, spread)
        for h in range(halves)
    ]
    gathered = [lax.all_gather(m, ("mode", "cores"), axis=0, tiled=False) for m in mixed]
    cols = None
    for h in range(halves):
        cols = rows_back(back_rows, gathered[h], channels, h, halves, cols)
    cols = cols.reshape(row_count, 2 * MY, channels)

    skip_wide = skip_weight.astype(jnp.float32)
    direct = jnp.dot(lift_weight.astype(jnp.float32), skip_wide, precision="highest")
    total_bias = jnp.dot(lift_bias, skip_wide, precision="highest") + skip_bias
    rows_eye = jnp.eye(HALF, dtype=jnp.float32)
    skip = (rows_eye[:, None, None, :] * direct.T[None, :, :, None]).astype(jnp.bfloat16)
    skip = skip.reshape(HALF * channels, variables * HALF)
    closing = out_weight.T[:, None, None, :] * rows_eye.astype(jnp.bfloat16)[None, :, :, None]
    closing = closing.reshape(variables * HALF, HALF * channels)
    bias = jnp.tile(total_bias, HALF)[:, None]
    last_bias = jnp.repeat(out_bias, HALF)[:, None]
    return finish(fields, cols, width, skip, bias, closing, last_bias)[None]


def solution(mesh):
    placed = (
        P("batch", None, ("mode", "cores"), None),
        P(),
        P(),
        P("batch", None, None),
        P(("mode", "cores"), None, None),
        P("batch", None, None),
        P("batch", None, None, None),
        P(),
        P(),
        P(),
        P(),
    )
    holders = mesh.shape["mode"] * mesh.shape["cores"]
    fits = MX // mesh.shape["batch"] % PACK == 0 and MY // holders % PACK == 0 and NX // holders % 128 == 0
    return jax.shard_map(
        fast_shards if fits else shards,
        mesh=mesh,
        in_specs=placed,
        out_specs=P("batch", None, ("mode", "cores"), None),
        check_vma=False,
    )
```

profile of v0, /device:TPU:0, one launch (start us, length us, event | category | flops | bytes accessed | tf_op | source)
XLA Modules:
  0.0 218.5 jit_solution(5945405289241396066)
XLA Ops:
  6.5 1.4 reshape.112
  11.1 4.2 %convolution_convert_fusion = bf16[256,20,128]{2,0,1:T(8,128)(2,1)S(1)} fusion(bf16[256,1024,1]{1,0,2:T(8,128)(2,1)} %constant.42, bf16[1,20,128,1024]{3,2,1,0:T(8,128)(2,1)} %param.17), kind=kOutput, calls=%fused_computation.1 | convolution fusion | flops 1342832640 | bytes 7077888 | tf_op jit(solution)/shard_map/ry,vxy->rvx/dot_general | solution.py:441
  16.3 1.7 reshape.108
  17.9 5.2 %all-to-all-start = ((bf16[8,32,2560]{2,1,0:T(8,128)(2,1)}), bf16[8,32,2560]{2,1,0:T(8,128)(2,1)S(1)}, u32[]{:S(2)}, u32[]{:S(2)}) async-start(bf16[8,32,2560]{2,1,0:T(8,128)(2,1)} %reshape.108), calls=%async_computation | async-start | bytes 2621440 | tf_op jit(solution)/shard_map/all_to_all | solution.py:445
  23.8 18.1 %all-gather.6.cloned.1.call-done = bf16[4,1024,128]{2,1,0:T(8,128)(2,1)} async-done(((bf16[1,1024,128]{2,1,0:T(8,128)(2,1)}), bf16[4,1024,128]{2,1,0:T(8,128)(2,1)}) %all-gather.6.cloned.1.call-update) | async-done | bytes 1048592 | tf_op jit(solution)/shard_map/all_gather | solution.py:397
  41.9 2.0 copy.56
  45.1 2.6 %reshape.114 = bf16[128,32,32]{2,1,0:T(8,128)(2,1)} reshape(bf16[4,32768]{1,0:T(4,128)(2,1)} %get-tuple-element.6) | data formatting | bytes 524288 | tf_op jit(solution)/shard_map/reshape | solution.py:402
  47.7 3.3 %copy.43 = bf16[128,32,32,1]{0,1,3,2:T(8,128)(2,1)} copy(bf16[128,32,32,1]{2,1,0,3:T(8,128)(2,1)} %bitcast.80) | data formatting | bytes 524288 | tf_op jit(solution)/shard_map/reshape | solution.py:402
  51.0 2.2 convert_bitcast_fusion
  53.2 4.7 %copy.36 = bf16[32,128,16,32]{1,3,2,0:T(8,128)(2,1)} copy(bf16[32,128,16,32]{1,0,2,3:T(8,128)(2,1)S(1)} %convert_bitcast_fusion) | data formatting | bytes 8388608 | tf_op jit(solution)/shard_map/convert_element_type | solution.py:456
  57.9 6.5 %copy.38.joined = bf16[32,128,512]{2,1,0:T(8,128)(2,1)} copy(bf16[32,128,512]{1,2,0:T(8,128)(2,1)} %bitcast.76) | data formatting | bytes 8388608 | tf_op jit(solution)/shard_map/reshape | solution.py:456
  64.3 2.7 %reshape.116.first = bf16[4096,32]{1,0:T(8,128)(2,1)} reshape(bf16[4,32768]{1,0:T(4,128)(2,1)} %get-tuple-element.5) | data formatting | bytes 524288 | tf_op jit(solution)/shard_map/reshape | solution.py:401
  67.0 2.6 %reshape.117 = bf16[128,2,32,32]{3,2,1,0:T(8,128)(2,1)} reshape(bf16[4,65536]{1,0:T(4,128)(2,1)S(1)} %slice.14) | data formatting | bytes 1048576 | tf_op jit(solution)/shard_map/reshape | solution.py:403
  69.6 4.5 %copy.37 = bf16[32,32,2,128]{3,2,1,0:T(2,128)(2,1)} copy(bf16[32,32,2,128]{0,1,2,3:T(8,128)(2,1)} %bitcast.77) | data formatting | bytes 1048576 | tf_op jit(solution)/shard_map/transpose | solution.py:457
  76.5 1.2 copy-done.6
  77.7 15.0 %mix.3 = bf16[256,1024]{1,0:T(8,128)(2,1)} custom-call(bf16[8,32,2560]{2,1,0:T(8,128)(2,1)S(1)} %all-to-all-done.arrived, bf16[256,2048]{1,0:T(8,128)(2,1)S(1)} %copy-done.6, bf16[320,2048]{1,0:T(8,128)(2,1)S(1)} %bitcast.69, f32[256,1]{1,0:T(8,128)S(1)} %copy-done.8, f32[1,2048]{1,0:T(1,128)S(1)} %bitcast.73, bf16[32,128,512]{2,1,0:T(8,128)(2,1)} %copy.38.joined, ...), custom_call_target="tpu_custom_call" | custom-call | flops 14000000000 | bytes 8388608 | tf_op jit(solution)/shard_map/mix/pallas_call | solution.py:267
  95.2 15.2 %mix.2 = bf16[256,1024]{1,0:T(8,128)(2,1)} custom-call(bf16[8,32,2560]{2,1,0:T(8,128)(2,1)S(1)} %all-to-all-done.arrived, bf16[256,2048]{1,0:T(8,128)(2,1)S(1)} %copy-done.7, bf16[320,2048]{1,0:T(8,128)(2,1)S(1)} %bitcast.70, f32[256,1]{1,0:T(8,128)S(1)} %copy-done.8, f32[1,2048]{1,0:T(1,128)S(1)} %bitcast.74, bf16[32,128,512]{2,1,0:T(8,128)(2,1)} %copy.38.joined, ...), custom_call_target="tpu_custom_call" | custom-call | flops 14000000000 | bytes 8388608 | tf_op jit(solution)/shard_map/mix/pallas_call | solution.py:267
  112.7 16.4 %all-gather.10.cloned.1.call-done = bf16[2048,1024]{1,0:T(8,128)(2,1)} async-done(((bf16[256,1024]{1,0:T(8,128)(2,1)}), bf16[2048,1024]{1,0:T(8,128)(2,1)}) %all-gather.10.cloned.1.call-update) | async-done | bytes 4194320 | tf_op jit(solution)/shard_map/all_gather | solution.py:467
  129.1 2.2 %copy-done.1 = bf16[2048,1024]{1,0:T(8,128)(2,1)S(1)} copy-done((bf16[2048,1024]{1,0:T(8,128)(2,1)S(1)}, bf16[2048,1024]{1,0:T(8,128)(2,1)}, u32[]{:S(2)}) %copy-start.1) | copy-done | bytes 4194328
  131.3 7.8 %rows_back.2.rest_0_ = bf16[128,2,128,128]{3,2,1,0:T(8,128)(2,1)} custom-call(bf16[256,256]{1,0:T(8,128)(2,1)S(1)} %dynamic-slice_bitcast_fusion.table, bf16[8,256,1024]{2,1,0:T(8,128)(2,1)S(1)} %bitcast.67), custom_call_target="tpu_custom_call" | custom-call | flops 1073741824 | bytes 16777216 | tf_op jit(solution)/shard_map/rows_back/pallas_call | solution.py:310
  139.1 28.7 %all-gather.8.cloned.1.call-done = bf16[2048,1024]{1,0:T(8,128)(2,1)} async-done(((bf16[256,1024]{1,0:T(8,128)(2,1)}), bf16[2048,1024]{1,0:T(8,128)(2,1)}) %all-gather.8.cloned.1.call-update) | async-done | bytes 4194320 | tf_op jit(solution)/shard_map/all_gather | solution.py:467
  167.7 2.2 %copy-done.2 = bf16[2048,1024]{1,0:T(8,128)(2,1)S(1)} copy-done((bf16[2048,1024]{1,0:T(8,128)(2,1)S(1)}, bf16[2048,1024]{1,0:T(8,128)(2,1)}, u32[]{:S(2)}) %copy-start.2) | copy-done | bytes 4194328
  169.9 7.8 %rows_back.3 = bf16[128,2,128,128]{3,2,1,0:T(8,128)(2,1)} custom-call(bf16[256,256]{1,0:T(8,128)(2,1)S(1)} %dynamic-slice_bitcast_fusion.table, bf16[8,256,1024]{2,1,0:T(8,128)(2,1)S(1)} %bitcast.68, bf16[128,2,128,128]{3,2,1,0:T(8,128)(2,1)} %rows_back.2.rest_0_), custom_call_target="tpu_custom_call", output_to_operand_aliasing={{}: (2, {})} | custom-call | flops 1073741824 | bytes 16777216 | tf_op jit(solution)/shard_map/rows_back/pallas_call | solution.py:310
  177.7 34.3 %finish.1 = bf16[20,128,1024]{2,1,0:T(8,128)(2,1)} custom-call(bf16[20,128,1024]{2,1,0:T(8,128)(2,1)} %bitcast.79, bf16[128,256,128]{2,1,0:T(8,128)(2,1)} %bitcast.75, bf16[256,1024]{1,0:T(8,128)(2,1)S(1)} %copy-done.5, bf16[1024,160]{1,0:T(8,128)(2,1)S(1)} %copy.40.skip, f32[1024,1]{1,0:T(8,128)S(1)} %copy.41.bias, ...), custom_call_target="tpu_custom_call" | custom-call | tf_op jit(solution)/shard_map/finish/pallas_call | solution.py:371
  (63 shorter events, 12.9 us)
Async XLA Ops:
  6.5 44.4 %copy-start = (bf16[16,32,32]{2,1,0:T(8,128)(2,1)S(1)}, bf16[16,32,32]{2,1,0:T(8,128)(2,1)}, u32[]{:S(2)}) copy-start(bf16[16,32,32]{2,1,0:T(8,128)(2,1)} %param.21) | copy-start | bytes 98308
  6.5 35.4 %all-gather.6.cloned.1.call-start = ((), (), s32[]{:S(2)}) async-start(), calls=%async_computation.1 | async-start | bytes 1310720 | tf_op jit(solution)/shard_map/all_gather | solution.py:397
  15.3 7.8 %copy-start.11 = (bf16[20,128]{1,0:T(8,128)(2,1)S(1)}, bf16[20,128]{1,0:T(8,128)(2,1)}, u32[]{:S(2)}) copy-start(bf16[20,128]{1,0:T(8,128)(2,1)} %param.18) | copy-start | bytes 15364
  16.2 7.5 %copy-start.14 = (f32[128]{0:T(128)S(1)}, f32[128]{0:T(128)}, u32[]{:S(2)}) copy-start(f32[128]{0:T(128)} %param.19) | copy-start | bytes 1540
  17.9 57.3 %all-to-all-start = ((bf16[8,32,2560]{2,1,0:T(8,128)(2,1)}), bf16[8,32,2560]{2,1,0:T(8,128)(2,1)S(1)}, u32[]{:S(2)}, u32[]{:S(2)}) async-start(bf16[8,32,2560]{2,1,0:T(8,128)(2,1)} %reshape.108), calls=%async_computation | async-start | bytes 2621440 | tf_op jit(solution)/shard_map/all_to_all | solution.py:445
  23.1 106.0 %all-gather.10.cloned.1.call-start = ((), (), s32[]{:S(2)}) async-start(), calls=%async_computation.3 | async-start | bytes 4718592 | tf_op jit(solution)/shard_map/all_gather | solution.py:467
  64.3 10.9 %copy-start.8 = (f32[256,1]{1,0:T(8,128)S(1)}, f32[256,1]{1,0:T(8,128)}, u32[]{:S(2)}) copy-start(f32[256,1]{1,0:T(8,128)} %constant.38.clone.row_sum) | copy-start | bytes 3076
  64.3 10.9 %copy-start.9 = (bf16[32,512]{1,0:T(8,128)(2,1)S(1)}, bf16[32,512]{1,0:T(8,128)(2,1)}, u32[]{:S(2)}) copy-start(bf16[32,512]{1,0:T(8,128)(2,1)} %constant.37.clone.spread) | copy-start | bytes 98308
  75.3 1.2 copy-start.3
  76.5 1.2 copy-start.6
  92.7 75.0 %all-gather.8.cloned.1.call-start = ((), (), s32[]{:S(2)}) async-start(), calls=%async_computation.2 | async-start | bytes 4718592 | tf_op jit(solution)/shard_map/all_gather | solution.py:467
  92.8 1.2 copy-start.4
  94.0 1.2 copy-start.7
  95.2 15.3 %copy-start.10 = (bf16[128,128]{1,0:T(8,128)(2,1)S(1)}, bf16[128,128]{1,0:T(8,128)(2,1)}, u32[]{:S(2)}) copy-start(bf16[128,128]{1,0:T(8,128)(2,1)} %param.24) | copy-start | bytes 98308
  95.2 15.8 %copy-start.15 = (f32[128]{0:T(128)S(1)}, f32[128]{0:T(128)}, u32[]{:S(2)}) copy-start(f32[128]{0:T(128)} %param.25) | copy-start | bytes 1540
  95.2 16.2 %copy-start.13 = (f32[20]{0:T(128)S(1)}, f32[20]{0:T(128)}, u32[]{:S(2)}) copy-start(f32[20]{0:T(128)} %param.27) | copy-start | bytes 244
  95.2 17.3 %copy-start.12 = (bf16[128,20]{0,1:T(8,128)(2,1)S(1)}, bf16[128,20]{0,1:T(8,128)(2,1)}, u32[]{:S(2)}) copy-start(bf16[128,20]{0,1:T(8,128)(2,1)} %param.26) | copy-start | bytes 15364
  129.1 2.2 %copy-start.1 = (bf16[2048,1024]{1,0:T(8,128)(2,1)S(1)}, bf16[2048,1024]{1,0:T(8,128)(2,1)}, u32[]{:S(2)}) copy-start(bf16[2048,1024]{1,0:T(8,128)(2,1)} %all-gather.10.cloned.1.call-done) | copy-start | bytes 12582916
  167.7 2.2 %copy-start.2 = (bf16[2048,1024]{1,0:T(8,128)(2,1)S(1)}, bf16[2048,1024]{1,0:T(8,128)(2,1)}, u32[]{:S(2)}) copy-start(bf16[2048,1024]{1,0:T(8,128)(2,1)} %all-gather.8.cloned.1.call-done) | copy-start | bytes 12582916
  169.9 7.8 %copy-start.5 = (bf16[256,1024]{1,0:T(8,128)(2,1)S(1)}, bf16[256,1024]{1,0:T(8,128)(2,1)}, u32[]{:S(2)}) copy-start(bf16[256,1024]{1,0:T(8,128)(2,1)} %constant.35.clone.width) | copy-start | bytes 1572868
Sparse Core Ops, SparseCore 0:
  11.2 30.6 all-gather.5
  92.8 36.1 all-gather.9
  131.0 36.7 all-gather.7
where the time goes:
time: 219 us; the launch traced here: 218 us
  Pallas kernels  80 us (37%)
  waiting for transfers between devices  63.2 us (29%)
  local copies, waits for them, and re-layouts  48.7 us (22%)
  between operations  13.4 us (6%)
  matrix products  6.67 us (3%)
  starting transfers between devices  5.25 us (2%)
    all_gather x2, waiting for transfers between devices, fast_shards(): lax.all_gather(m, ('mode', 'cores'), axis=0, tiled=False)  45.1 us
    pallas_call x1, Pallas kernels, finish(): pl.pallas_call(finish_kernel, grid=(row_count // PACK,), in_specs=[pl.Blo...  34.3 us
    pallas_call x2, Pallas kernels, mix(): pl.pallas_call(functools.partial(mix_kernel, base), grid=(groups,), in_sp...  30.2 us
    all_gather x1, waiting for transfers between devices, gather_factors(): whole = lax.all_gather(flat, 'batch', axis=0, tiled=False)  18.1 us
    pallas_call x2, Pallas kernels, rows_back(): pl.pallas_call(rows_kernel, grid=(holders,), in_specs=[pl.BlockSpec(table...  15.6 us
    unnamed x36, local copies, waits for them, and re-layouts  12.9 us
    reshape x1, local copies, waits for them, and re-layouts, fast_shards(): joined = jnp.einsum('mbd,cde->bcme', second_core, inner, preferred_elemen...  6.46 us
    reshape x2, local copies, waits for them, and re-layouts, gather_factors(): inner = whole[:, size:2 * size].reshape(parts * count, rank, rank)  5.85 us
  transfers between devices with their start and end apart: 4, of which 3 were waited for; matrix products, arithmetic and copies ran while one was open for 20% of the time, Pallas kernels for 11%

commit v1 on v0

v1 whole, which is shorter than its diff:
```python
import functools
import math

import jax
import jax.numpy as jnp
import ml_dtypes
import numpy as np
from jax import lax
from jax.experimental import pallas as pl
from jax.experimental.pallas import tpu as pltpu
from jax.sharding import PartitionSpec as P

NX = 1024
NY = 1024
MX = 128
MY = 128


TWO_PI = 2.0 * math.pi


def wave_pair(waves, points, length):
    phase_step = waves[:, None] * points[None, :] % length
    angles = phase_step.astype(jnp.float32) * (TWO_PI / length)
    return (jnp.cos(angles), jnp.sin(angles))


def width_forward(length, wave_count):
    points = jnp.arange(length, dtype=jnp.int32)
    waves = jnp.arange(wave_count, dtype=jnp.int32)
    cosines, sine_part = wave_pair(points, waves, length)
    stacked = jnp.stack([cosines, -sine_part], axis=1) / math.sqrt(length)
    return stacked.astype(jnp.bfloat16)


def height_forward(row_index, wave_count, length):
    waves = jnp.arange(wave_count, dtype=jnp.int32) - wave_count // 2
    cosines, sine_part = wave_pair(waves, row_index, length)
    upper = jnp.stack([cosines, sine_part], axis=1)
    lower = jnp.stack([-sine_part, cosines], axis=1)
    return (jnp.stack([upper, lower], axis=0) / math.sqrt(length)).astype(jnp.bfloat16)


def height_inverse(row_index, wave_count, length):
    waves = jnp.arange(wave_count, dtype=jnp.int32) - wave_count // 2
    cosines, sine_part = wave_pair(row_index, waves, length)
    upper = jnp.stack([cosines, -sine_part], axis=1)
    lower = jnp.stack([sine_part, cosines], axis=1)
    return (jnp.stack([upper, lower], axis=0) / math.sqrt(length)).astype(jnp.bfloat16)


def width_inverse(waves, length):
    points = jnp.arange(length, dtype=jnp.int32)
    cosines, sine_part = wave_pair(waves, points, length)
    weight = jnp.where(waves == 0, 1.0, 2.0).astype(jnp.float32)[:, None]
    stacked = jnp.stack([cosines * weight, -sine_part * weight], axis=0) / math.sqrt(length)
    return stacked.astype(jnp.bfloat16)


def bias_modes(lift_bias, wave_index, length):
    real_row = (
        jnp.where(wave_index == 0, 1.0, 0.0).astype(jnp.float32)[:, None]
        * (math.sqrt(length) * lift_bias)[None, :]
    )
    return jnp.stack([real_row, jnp.zeros_like(real_row)], axis=0)


def lift_modes(modes, lift_weight, lift_bias, wave_index):
    lifted_modes = jnp.einsum(
        "fabpmv,vc->fabpmc", modes, lift_weight, preferred_element_type=jnp.float32
    )
    return (lifted_modes + bias_modes(lift_bias, wave_index, NY)).astype(jnp.bfloat16)


def grid_rows(stored, row_count, holder_count):
    return stored % row_count * holder_count + stored // row_count


def shards(
    fields,
    lift_weight,
    lift_bias,
    first_core,
    second_core,
    input_core,
    output_core,
    skip_weight,
    skip_bias,
    out_weight,
    out_bias,
):
    mode_count = lax.axis_size("mode")
    core_count = lax.axis_size("cores")
    row_count = fields.shape[2]
    block_size = second_core.shape[0]
    block_start = (lax.axis_index("mode") * core_count + lax.axis_index("cores")) * block_size
    local_waves = block_start + jnp.arange(block_size, dtype=jnp.int32)
    lifted = (
        jnp.einsum("fvxy,vc->fxyc", fields, lift_weight, preferred_element_type=jnp.float32)
        + lift_bias
    ).astype(jnp.bfloat16)
    field_modes = jnp.einsum(
        "fvxy,ypk->fxpkv", fields, width_forward(NY, MY), preferred_element_type=jnp.float32
    ).astype(jnp.bfloat16)
    field_modes = field_modes[:, None]
    gathered = (
        lax.all_gather(first_core, "batch", axis=0, tiled=True),
        lax.all_gather(input_core, "batch", axis=0, tiled=True),
        lax.all_gather(output_core, "batch", axis=0, tiled=True),
    )
    first_whole, input_whole, output_whole = gathered
    mode_factor = jnp.einsum(
        "kab,mbd->kmad", first_whole, second_core, preferred_element_type=jnp.float32
    ).astype(jnp.bfloat16)
    arrived = lax.all_to_all(
        field_modes, ("mode", "cores"), split_axis=4, concat_axis=2, tiled=True
    )
    rows_held = jnp.arange(NX, dtype=jnp.int32)[None, :]
    by_mode = lift_modes(arrived, lift_weight, lift_bias, local_waves)
    lead_rows = rows_held.shape[0]
    side_rows = rows_held.shape[1]
    flat_rows = grid_rows(rows_held.reshape(-1), row_count, mode_count * core_count)
    height_table = height_forward(flat_rows, MX, NX).reshape(2, MX, 2, lead_rows, side_rows)
    spectrum = jnp.einsum(
        "qkpab,fabpmc->fqkmc", height_table, by_mode, preferred_element_type=jnp.float32
    ).astype(jnp.bfloat16)
    projected = jnp.einsum(
        "fqkmc,cbe->fqkmbe", spectrum, input_whole, preferred_element_type=jnp.float32
    ).astype(jnp.bfloat16)
    carried = jnp.einsum(
        "kmab,fqkmbe->fqkmae", mode_factor, projected, preferred_element_type=jnp.float32
    ).astype(jnp.bfloat16)
    traced = jnp.einsum(
        "fqkmae,osea->fqkmso", carried, output_whole, preferred_element_type=jnp.float32
    )
    real_part = traced[:, 0, :, :, 0, :] - traced[:, 1, :, :, 1, :]
    imaginary = traced[:, 0, :, :, 1, :] + traced[:, 1, :, :, 0, :]
    mixed_modes = jnp.stack([real_part, imaginary], axis=1).astype(jnp.bfloat16)
    height_back = height_inverse(flat_rows, MX, NX).reshape(2, lead_rows, side_rows, 2, MX)
    col_modes = jnp.einsum(
        "pabqk,fqkmc->fabpmc", height_back, mixed_modes, preferred_element_type=jnp.float32
    ).astype(jnp.bfloat16)
    returned = lax.all_to_all(col_modes, ("mode", "cores"), split_axis=2, concat_axis=4, tiled=True)
    waves_held = jnp.arange(MY, dtype=jnp.int32)
    width_back = width_inverse(waves_held, NY)
    spatial = jnp.einsum(
        "fxpmc,pmy->fxyc", returned[:, 0], width_back, preferred_element_type=jnp.float32
    )
    skip_term = jnp.einsum("fxyc,cd->fxyd", lifted, skip_weight, preferred_element_type=jnp.float32)
    active = jax.nn.gelu(spatial + skip_term + skip_bias, approximate=False).astype(jnp.bfloat16)
    result = (
        jnp.einsum("fxyc,cv->fvxy", active, out_weight, preferred_element_type=jnp.float32)
        + out_bias[:, None, None]
    )
    return result.astype(jnp.bfloat16)


def cyclic_rows(row_count, holders):
    return (np.arange(row_count)[None, :] * holders + np.arange(holders)[:, None]).reshape(-1)


def host_pair(waves, points, length):
    steps = np.asarray(waves)[:, None] * np.asarray(points)[None, :] % length
    angles = steps.astype(np.float32) * np.float32(TWO_PI / length)
    return np.cos(angles), np.sin(angles)


def dense(a, b, contract=((1,), (0,))):
    return lax.dot_general(a, b, (contract, ((), ())), preferred_element_type=jnp.float32)


MESH = pl.DeviceIdType.MESH
WAVES = 16
SLOTS = 32
EIGHT = 8
CHUNKS = 4
LANES = 512


def whole(a):
    return pl.BlockSpec(a.shape, lambda *_: (0,) * a.ndim)


def mix_kernel(
    arrived, height, place, bias_modes_row, inner, second, first, first_spread, outer, spread,
    mixed, stacked, placed, inner_wide, turned_inner, weights, rows, blocks, closing, carried, turned,
):
    holders, lead, flat = arrived.shape
    waves = lead // 2
    variables = stacked.shape[0] // waves
    row_count = flat // variables
    kx_count = height.shape[0] // 2
    rank = first.shape[1]
    channels = outer.shape[0] // 2
    pairs = waves // 2
    wide = 4 * rank
    slots = inner.shape[1] // rank
    packs = kx_count // EIGHT

    for d in range(holders):
        for p in range(2):
            for v in range(variables):
                stacked[v * waves:(v + 1) * waves, (d * 2 + p) * row_count:(d * 2 + p + 1) * row_count] = (
                    arrived[d, p * waves:(p + 1) * waves, v * row_count:(v + 1) * row_count]
                )
    by = dense(height[...], stacked[...], ((1,), (1,))).astype(jnp.bfloat16)
    placed[...] = (
        dense(by[:kx_count], place[0]) + dense(by[kx_count:], place[1]) + bias_modes_row[...]
    ).astype(jnp.bfloat16)

    for part in range(slots // 4):
        inner_wide[:, part * 4 * wide:(part + 1) * 4 * wide] = dense(
            inner[:, part * wide:(part + 1) * wide], spread[:wide, :4 * wide]
        ).astype(jnp.bfloat16)

    down = lax.broadcasted_iota(jnp.int32, (rank * EIGHT, rank * EIGHT), 0) % EIGHT
    across = lax.broadcasted_iota(jnp.int32, (rank * EIGHT, rank * EIGHT), 1) % EIGHT
    same = down == across

    def block_step(k, carry):
        start = pl.multiple_of(k * rank * EIGHT, rank * EIGHT)
        full = dense(first[pl.ds(start, rank * EIGHT), :], first_spread[...])
        blocks[k] = jnp.where(same, full, 0.0).astype(jnp.bfloat16)
        return carry

    lax.fori_loop(0, packs, block_step, 0)

    lanes = lax.broadcasted_iota(jnp.int32, (channels, 8 * wide), 1)
    part_of = lanes // rank % 2
    wave_of = lanes // (2 * rank) % 2
    for part in range(rank // 8):
        real = dense(outer[:channels, part * 8 * rank:(part + 1) * 8 * rank], spread[...])
        imaginary = dense(outer[channels:, part * 8 * rank:(part + 1) * 8 * rank], spread[...])
        for r in range(2):
            value = jnp.where(part_of == 0, imaginary, real) if r else jnp.where(part_of == 0, real, -imaginary)
            for m in range(2):
                closing[(m * 2 + r) * channels:(m * 2 + r + 1) * channels, part * 8 * wide:(part + 1) * 8 * wide] = (
                    jnp.where(wave_of == m, value, 0.0).astype(jnp.bfloat16)
                )

    turned_inner[...] = jnp.zeros_like(turned_inner)
    group_of = lax.broadcasted_iota(jnp.int32, (SLOTS, wide), 1) // rank

    def pair_step(j, carry):
        start = pl.multiple_of(j * 2 * rank, 2 * rank)
        column = pl.ds(pl.multiple_of(j * wide, wide), wide)
        joined = dense(second[pl.ds(start, 2 * rank), :], inner_wide[...])
        for m in range(2):
            for v in range(slots):
                turned_inner[m, :, v, :] = joined[m * rank:(m + 1) * rank, v * wide:(v + 1) * wide]
        for m in range(2):
            for b in range(rank):
                value = turned_inner[m, b]
                for q in range(2):
                    weights[(q * 2 + m) * SLOTS:(q * 2 + m + 1) * SLOTS, b * wide:(b + 1) * wide] = jnp.where(
                        group_of == m * 2 + q, value, 0.0
                    ).astype(jnp.bfloat16)
        own = placed[:, column]
        for part in range(rank // 8):
            got = dense(own, weights[:, part * 8 * wide:(part + 1) * 8 * wide])
            for k in range(packs):
                rows[k, part * 64:(part + 1) * 64, column] = jnp.concatenate(
                    [got[k * EIGHT:(k + 1) * EIGHT, b * wide:(b + 1) * wide] for b in range(8)], axis=0
                ).astype(jnp.bfloat16)
        return carry

    lax.fori_loop(0, pairs, pair_step, 0)

    def first_step(k, carry):
        here = pl.ds(pl.multiple_of(k * 2 * EIGHT, 2 * EIGHT), 2 * EIGHT)
        for part in range(pairs // 2):
            one, two = [
                dense(blocks[2 * k + i], rows[2 * k + i, :, part * 2 * wide:(part + 1) * 2 * wide]) for i in range(2)
            ]
            for j in range(2):
                side = slice(j * wide, (j + 1) * wide)
                for a in range(rank):
                    level = slice(a * EIGHT, (a + 1) * EIGHT)
                    carried[part * 2 + j, here, a * wide:(a + 1) * wide] = jnp.concatenate(
                        [one[level, side], two[level, side]], axis=0
                    ).astype(jnp.bfloat16)
        return carry

    lax.fori_loop(0, packs // 2, first_step, 0)

    for part in range(pairs // 2):
        both = carried[part * 2:part * 2 + 2].reshape(2 * kx_count, rank * wide)
        got = dense(closing[...], both, ((1,), (1,)))
        for m in range(2):
            for r in range(2):
                for j in range(2):
                    turned[:, (part * 2 + j) * 2 + m, r * kx_count:(r + 1) * kx_count] = got[
                        (m * 2 + r) * channels:(m * 2 + r + 1) * channels, j * kx_count:(j + 1) * kx_count
                    ]
    mixed[...] = turned[...].astype(jnp.bfloat16)


def mix(arrived, height, place, bias_row, inner, second, first, first_spread, outer, spread):
    holders, lead, flat = arrived.shape
    waves = lead // 2
    kx2, depth = height.shape
    rank = first.shape[1]
    channels = outer.shape[0] // 2
    wide = 4 * rank
    slots = inner.shape[1] // rank
    packs = kx2 // 2 // EIGHT
    operands = (arrived, height, place, bias_row, inner, second, first, first_spread, outer, spread)
    return pl.pallas_call(
        mix_kernel,
        in_specs=[pl.BlockSpec(memory_space=pltpu.VMEM) for _ in operands],
        out_specs=pl.BlockSpec(memory_space=pltpu.VMEM),
        out_shape=jax.ShapeDtypeStruct((channels, waves, kx2), jnp.bfloat16),
        scratch_shapes=[
            pltpu.VMEM((place.shape[1], depth), jnp.bfloat16),
            pltpu.VMEM((kx2 // 2, waves // 2 * wide), jnp.bfloat16),
            pltpu.VMEM((rank, slots * wide), jnp.bfloat16),
            pltpu.VMEM((2, rank, SLOTS, wide), jnp.float32),
            pltpu.VMEM((4 * SLOTS, rank * wide), jnp.bfloat16),
            pltpu.VMEM((packs, rank * EIGHT, waves // 2 * wide), jnp.bfloat16),
            pltpu.VMEM((packs, rank * EIGHT, rank * EIGHT), jnp.bfloat16),
            pltpu.VMEM((4 * channels, rank * wide), jnp.bfloat16),
            pltpu.VMEM((waves // 2, kx2 // 2, rank * wide), jnp.bfloat16),
            pltpu.VMEM((channels, waves, kx2), jnp.float32),
        ],
        compiler_params=pltpu.CompilerParams(vmem_limit_bytes=56 * 2**20),
        name="mix",
    )(*operands)


def gelu(h):
    return h * (0.5 + 0.5 * lax.erf(h * (1.0 / math.sqrt(2.0))))


def finish_kernel(
    mixed, back, fields, width, skip, bias, closing, out_bias,
    result, gathered, source, cols, total, send, recv,
):
    channels, waves, kx2 = mixed.shape
    variables, row_count, points = fields.shape
    share = channels // CHUNKS
    depth = share * EIGHT
    half = share // 2
    mode, batch, core = lax.axis_index("mode"), lax.axis_index("batch"), lax.axis_index("cores")
    near = (mode + 1 - 2 * (mode % 2), batch, core)
    by_x = ((mode + 2) % 4, batch, core)
    by_y = (mode, batch, 1 - core)

    def owner(device):
        return device[0] * 2 + device[2]

    me = owner((mode, batch, core))
    at_x, at_y = owner(by_x), owner(by_y)
    across = owner((by_x[0], batch, by_y[2]))

    barrier = pltpu.get_barrier_semaphore()
    for device in (near, by_x, by_y):
        pl.semaphore_signal(barrier, inc=1, device_id=device, device_id_type=MESH)
    pl.semaphore_wait(barrier, 3)

    def piece(holder, first, count):
        return gathered.at[pl.ds(first, count), pl.ds(pl.multiple_of(holder * waves, waves), waves), :]

    def copy(g, kind):
        low = g * share
        own = mixed.at[pl.ds(low, share)]
        home = piece(me, low, share)
        x_all, y_all = piece(at_x, low, share), piece(at_y, low, share)
        x_low, y_high = piece(at_x, low, half), piece(at_y, low + half, half)
        d_low, d_high = piece(across, low, half), piece(across, low + half, half)
        from_, to, device = (
            (own, home, near), (own, home, by_x), (own, home, by_y),
            (x_all, x_all, near), (y_all, y_all, near),
            (x_low, x_low, by_y), (y_high, y_high, by_x),
            (d_low, d_low, near), (d_high, d_high, near),
        )[kind]
        return pltpu.make_async_remote_copy(
            src_ref=from_, dst_ref=to, send_sem=send.at[g, kind], recv_sem=recv.at[g, kind],
            device_id=device, device_id_type=MESH,
        )

    def begin(g, kinds):
        for kind in kinds:
            copy(g, kind).start()

    def came(g, kinds):
        for kind in kinds:
            copy(g, kind).wait_recv()

    def relay(g):
        came(g, (1, 2))
        begin(g, (5, 6, 3, 4))
        if g + 1 < CHUNKS:
            begin(g + 1, (1, 2, 0))

    def relay_last(g):
        came(g, (5, 6))
        begin(g, (7, 8))

    begin(0, (1, 2, 0))
    gathered[:, pl.ds(pl.multiple_of(me * waves, waves), waves), :] = mixed[...]
    for x in range(row_count // EIGHT // 2):
        rows = fields[:, x * 2 * EIGHT:(x + 1) * 2 * EIGHT, :]
        for h in range(2):
            source[x * 2 + h] = rows[:, h * EIGHT:(h + 1) * EIGHT, :].reshape(variables * EIGHT, points)
    relay(0)
    relay_last(0)

    def turn(g):
        def step(c, carry):
            both = gathered[pl.ds(g * share + 2 * c, 2)].reshape(2 * waves * 8, kx2)
            got = dense(back[...], both, ((1,), (1,)))
            place = pl.ds(pl.multiple_of(c * 2 * EIGHT, 2 * EIGHT), 2 * EIGHT)
            size = got.shape[1] // 2
            for p in range(2):
                for x in range(row_count // EIGHT):
                    rows = got[p * row_count + x * EIGHT:p * row_count + (x + 1) * EIGHT, :]
                    cols[x, place, p * size:(p + 1) * size] = jnp.concatenate(
                        [rows[:, :size], rows[:, size:]], axis=0
                    ).astype(jnp.bfloat16)
            return carry

        lax.fori_loop(0, share // 2, step, 0)

    def finish_rows(g, low, high):
        part = slice(g * depth, (g + 1) * depth)

        def step(i, carry):
            for lane in range(points // LANES):
                lanes = slice(lane * LANES, (lane + 1) * LANES)
                done = []
                for h in range(2):
                    x = 2 * i + h
                    height = (
                        dense(cols[x], width[:, lanes]) + dense(skip[part, :], source[x, :, lanes]) + bias[part, :]
                    )
                    active = gelu(height).astype(jnp.bfloat16)
                    got = dense(closing[:, part], active)
                    got = got + (out_bias[...] if g == 0 else total[x, :, lanes])
                    if g + 1 < CHUNKS:
                        total[x, :, lanes] = got
                    else:
                        done.append(got.reshape(variables, EIGHT, LANES))
                if done:
                    place = pl.ds(pl.multiple_of(i * 2 * EIGHT, 2 * EIGHT), 2 * EIGHT)
                    result[:, place, lanes] = jnp.concatenate(done, axis=1).astype(jnp.bfloat16)
            return carry

        lax.fori_loop(low, high, step, 0)

    steps = row_count // EIGHT // 2
    for g in range(CHUNKS):
        came(g, (0, 3, 4, 7, 8))
        turn(g)
        if g + 1 < CHUNKS:
            finish_rows(g, 0, steps // 4)
            relay(g + 1)
            finish_rows(g, steps // 4, 5 * steps // 8)
            relay_last(g + 1)
            finish_rows(g, 5 * steps // 8, steps)
        else:
            finish_rows(g, 0, steps)
    for g in range(CHUNKS):
        for kind in range(9):
            copy(g, kind).wait_send()


def finish(mixed, back, fields, width, skip, bias, closing, out_bias):
    channels, waves, kx2 = mixed.shape
    variables, row_count, points = fields.shape
    operands = (mixed, back, fields, width, skip, bias, closing, out_bias)
    share = channels // CHUNKS
    blocks = row_count // EIGHT
    return pl.pallas_call(
        finish_kernel,
        in_specs=[pl.BlockSpec(memory_space=pltpu.VMEM) for _ in operands],
        out_specs=pl.BlockSpec(memory_space=pltpu.VMEM),
        out_shape=jax.ShapeDtypeStruct(fields.shape, jnp.bfloat16),
        scratch_shapes=[
            pltpu.VMEM((channels, 8 * waves, kx2), jnp.bfloat16),
            pltpu.VMEM((blocks, variables * EIGHT, points), jnp.bfloat16),
            pltpu.VMEM((blocks, share * EIGHT, width.shape[0]), jnp.bfloat16),
            pltpu.VMEM((blocks, variables * EIGHT, points), jnp.float32),
            pltpu.SemaphoreType.DMA((CHUNKS, 9)),
            pltpu.SemaphoreType.DMA((CHUNKS, 9)),
        ],
        compiler_params=pltpu.CompilerParams(
            collective_id=0, has_side_effects=True, vmem_limit_bytes=60 * 2**20
        ),
        name="finish",
    )(*operands)


def gather_factors(first_core, input_core, output_core):
    count, rank, _ = first_core.shape
    first_core = first_core.reshape(count // EIGHT, EIGHT, rank, rank).transpose(0, 2, 1, 3)
    output_core = output_core.transpose(1, 0, 3, 2)
    flat = jnp.concatenate(
        [first_core.reshape(-1), input_core.reshape(-1), output_core.reshape(-1)]
    ).reshape(-1, 128)
    gathered = lax.all_gather(flat, "batch", axis=0, tiled=False)
    parts = gathered.shape[0]
    size = first_core.size
    gathered = gathered.reshape(parts, -1)
    first = gathered[:, :size].reshape(-1, rank)
    inner = gathered[:, size:2 * size].reshape(parts * count, rank * rank)
    outer = gathered[:, 2 * size:].reshape(parts, 2, count, rank * rank).transpose(1, 0, 2, 3)
    return first, inner, outer.reshape(2 * parts * count, rank * rank)


def fast_shards(
    fields, lift_weight, lift_bias, first_core, second_core, input_core, output_core,
    skip_weight, skip_bias, out_weight, out_bias,
):
    holders = lax.axis_size("mode") * lax.axis_size("cores")
    waves, rank, _ = second_core.shape
    _, variables, row_count, points = fields.shape
    channels = lift_weight.shape[1]
    fields = fields[0]
    me = lax.axis_index("mode") * lax.axis_size("cores") + lax.axis_index("cores")

    cosines, sines = host_pair(np.arange(MY), np.arange(points), points)
    root = math.sqrt(points)
    forward = np.stack([cosines, -sines], 0).reshape(2, holders, waves, points).transpose(1, 0, 2, 3)
    forward = jnp.asarray((forward.reshape(2 * MY, points) / root).astype(np.float32)).astype(jnp.bfloat16)
    weight = np.where(np.arange(MY) == 0, 1.0, 2.0).astype(np.float32)[:, None]
    width = np.concatenate([cosines * weight, -sines * weight], 0) / root
    width = jnp.asarray(width.astype(ml_dtypes.bfloat16))
    order = cyclic_rows(row_count, holders)
    root = math.sqrt(NX)
    cosines, sines = host_pair(np.arange(MX) - MX // 2, order, NX)
    cosines, sines = [t.reshape(MX, holders, row_count) / root for t in (cosines, sines)]
    upper = np.stack([cosines, sines], 2)
    lower = np.stack([-sines, cosines], 2)
    height = np.stack([upper, lower], 0).reshape(2 * MX, -1).astype(ml_dtypes.bfloat16)
    real_part = np.asarray(height, np.float32).reshape(2 * MX, holders, 2, row_count)[:, :, 0]
    row_sum = real_part.sum((1, 2), dtype=np.float64).astype(np.float32)
    cos_t, sin_t = [t.transpose(1, 2, 0) for t in (cosines, sines)]
    up = np.concatenate([cos_t, -sin_t], 2)
    low = np.concatenate([sin_t, cos_t], 2)
    back_rows = jnp.asarray(np.concatenate([up, low], 1).astype(ml_dtypes.bfloat16))
    back_rows = lax.dynamic_index_in_dim(back_rows, me, 0, keepdims=False)
    pairs = waves // 2
    place = np.zeros((2, variables, waves, pairs, 2, 2, SLOTS), np.float32)
    for q in range(2):
        for v in range(variables):
            for m in range(waves):
                place[q, v, m, m // 2, q, m % 2, v] = 1.0
    place = jnp.asarray(place.reshape(2, variables * waves, -1).astype(ml_dtypes.bfloat16))
    bias_row = np.zeros((MX, pairs, 2, 2, SLOTS), np.float32)
    bias_row[:, 0, :, 0, variables] = row_sum.reshape(2, MX).T
    bias_row = jnp.asarray(bias_row.reshape(MX, -1)) * (me == 0).astype(jnp.float32)
    first_spread = jnp.asarray(np.repeat(np.eye(rank), EIGHT, axis=1).astype(ml_dtypes.bfloat16))
    spread = np.eye(8)[:, None, :, None, None] * np.eye(rank)[None, :, None, None, :] * np.ones((1, 1, 1, 4, 1))
    spread = jnp.asarray(spread.reshape(8 * rank, 32 * rank).astype(ml_dtypes.bfloat16))

    first, inner, outer = gather_factors(first_core, input_core, output_core)
    modes = jnp.einsum(
        "ry,vxy->rvx", forward, fields, preferred_element_type=jnp.float32
    ).astype(jnp.bfloat16)
    modes = modes.reshape(holders, 2 * waves, variables * row_count)
    arrived = lax.all_to_all(modes, ("mode", "cores"), split_axis=0, concat_axis=0, tiled=True)

    used = (variables + 4) // 4 * 4
    lift = jnp.concatenate(
        [lift_weight, (math.sqrt(points) * lift_bias).astype(jnp.bfloat16)[None],
         jnp.zeros((used - variables - 1, channels), jnp.bfloat16)], 0
    )
    inner = jnp.einsum(
        "vc,cde->dve", lift, inner.reshape(channels, rank, rank), preferred_element_type=jnp.float32
    ).astype(jnp.bfloat16).reshape(rank, used * rank)
    mixed = mix(
        arrived, jnp.asarray(height), place, bias_row, inner, second_core.reshape(waves * rank, rank),
        first, first_spread, outer, spread,
    )

    skip_wide = skip_weight.astype(jnp.float32)
    direct = jnp.dot(lift_weight.astype(jnp.float32), skip_wide, precision="highest")
    total_bias = jnp.dot(lift_bias, skip_wide, precision="highest") + skip_bias
    rows_eye = jnp.eye(EIGHT, dtype=jnp.float32)
    skip = (direct.T[:, None, :, None] * rows_eye[None, :, None, :]).astype(jnp.bfloat16)
    skip = skip.reshape(channels * EIGHT, variables * EIGHT)
    closing = out_weight.T[:, None, :, None] * rows_eye.astype(jnp.bfloat16)[None, :, None, :]
    closing = closing.reshape(variables * EIGHT, channels * EIGHT)
    bias = jnp.repeat(total_bias, EIGHT)[:, None]
    last_bias = jnp.repeat(out_bias, EIGHT)[:, None]
    return finish(mixed, back_rows, fields, width, skip, bias, closing, last_bias)[None]


def solution(mesh):
    placed = (
        P("batch", None, ("mode", "cores"), None),
        P(),
        P(),
        P("batch", None, None),
        P(("mode", "cores"), None, None),
        P("batch", None, None),
        P("batch", None, None, None),
        P(),
        P(),
        P(),
        P(),
    )
    fits = (
        mesh.shape["mode"] == 4 and mesh.shape["cores"] == 2 and MY // 8 == WAVES
        and MX // mesh.shape["batch"] % EIGHT == 0 and NX // 8 == 128
    )
    return jax.shard_map(
        fast_shards if fits else shards,
        mesh=mesh,
        in_specs=placed,
        out_specs=P("batch", None, ("mode", "cores"), None),
        check_vma=False,
    )
```

time: 219 us -> 190 us (0.87)
  waiting for transfers between devices: 63.2 us -> 0.02 us
  Pallas kernels: 80 us -> 114 us
  local copies, waits for them, and re-layouts: 48.7 us -> 41.7 us
  other arithmetic: 1.24 us -> 8.14 us
    all_gather x3 -> x1, waiting for transfers between devices: 63.2 us -> 0.01 us  [gather_factors(): gathered = lax.all_gather(flat, 'batch', axis=0, tiled=False)]
    pallas_call x5 -> x2, Pallas kernels: 80 us -> 114 us  [the longest x1 87.7 us: finish(): pl.pallas_call(finish_kernel, in_specs=[pl.BlockSpec(memory_space=pltpu.V...]
    reshape x6 -> x3, local copies, waits for them, and re-layouts: 18.6 us -> 3.35 us  [the longest x1 1.53 us: gather_factors(): first = gathered[:, :size].reshape(-1, rank)]
    mul x0 -> x1, local copies, waits for them, and re-layouts: none -> 9.1 us  [fast_shards(): out_weight.T[:, None, :, None]]
    convert_element_type x2 -> x3, local copies, waits for them, and re-layouts: 4.92 us -> 9.55 us  [the longest x2 9.48 us: fast_shards(): (direct.T[:, None, :, None] * rows_eye[None, :, None, :]).astype(jnp.bflo...]
    unnamed x36 -> x19, local copies, waits for them, and re-layouts: 12.9 us -> 8.94 us
    convert_element_type x5 -> x3, other arithmetic: 0.03 us -> 3.77 us  [the longest x1 3.76 us: fast_shards(): (direct.T[:, None, :, None] * rows_eye[None, :, None, :]).astype(jnp.bflo...]
    mul x3 -> x2, other arithmetic: 0.35 us -> 3.62 us  [the longest x1 2.77 us: fast_shards(): out_weight.T[:, None, :, None]]
  transfers between devices with their start and end apart: 4 -> 2, of which waited for: 3 -> 0; matrix products, arithmetic and copies ran while one was open for 20% -> 23% of each run, Pallas kernels for 11% -> 0%
where the time goes in v1:
time: 190 us; the launch traced here: 188 us
  Pallas kernels  114 us (60%)
  local copies, waits for them, and re-layouts  41.7 us (22%)
  between operations  13.5 us (7%)
  other arithmetic  8.14 us (4%)
  starting transfers between devices  5.17 us (3%)
  matrix products  4.87 us (3%)
    pallas_call x1, Pallas kernels, finish(): pl.pallas_call(finish_kernel, in_specs=[pl.BlockSpec(memory_space=pltpu.V...  87.7 us
    pallas_call x1, Pallas kernels, mix(): pl.pallas_call(mix_kernel, in_specs=[pl.BlockSpec(memory_space=pltpu.VMEM...  26.8 us
    convert_element_type x2, local copies, waits for them, and re-layouts, fast_shards(): (direct.T[:, None, :, None] * rows_eye[None, :, None, :]).astype(jnp.bflo...  9.48 us
    mul x1, local copies, waits for them, and re-layouts, fast_shards(): out_weight.T[:, None, :, None]  9.1 us
    unnamed x19, local copies, waits for them, and re-layouts  8.94 us
    all_to_all x1, starting transfers between devices, fast_shards(): lax.all_to_all(modes, ('mode', 'cores'), split_axis=0, concat_axis=0, til...  5.17 us
    dot_general x1, matrix products, fast_shards(): jnp.einsum('ry,vxy->rvx', forward, fields, preferred_element_type=jnp.flo...  4.22 us
  transfers between devices with their start and end apart: 2, of which 0 were waited for; matrix products, arithmetic and copies ran while one was open for 23% of the time, Pallas kernels for 0%

profile of v1, /device:TPU:0, one launch (start us, length us, event | category | flops | bytes accessed | tf_op | source)
XLA Modules:
  0.0 187.9 jit_solution(13472027671916594757)
XLA Ops:
  6.5 1.2 reshape.60
  7.7 1.1 copy.47
  8.9 1.3 copy.33
  10.5 0.7 maximum_bitcast_fusion
  11.3 4.2 %convolution_convert_fusion = bf16[256,20,128]{2,0,1:T(8,128)(2,1)S(1)} fusion(bf16[256,1024,1]{1,0,2:T(8,128)(2,1)} %constant.48, bf16[1,20,128,1024]{3,2,1,0:T(8,128)(2,1)} %param.19), kind=kOutput, calls=%fused_computation.2 | convolution fusion | flops 1342832640 | bytes 7077888 | tf_op jit(solution)/shard_map/ry,vxy->rvx/dot_general | solution.py:557
  15.6 0.9 copy.31
  16.5 1.6 reshape.57
  18.1 5.2 %all-to-all-start = ((bf16[8,32,2560]{2,1,0:T(8,128)(2,1)}), bf16[8,32,2560]{2,1,0:T(8,128)(2,1)S(1)}, u32[]{:S(2)}, u32[]{:S(2)}) async-start(bf16[8,32,2560]{2,1,0:T(8,128)(2,1)} %reshape.57), calls=%async_computation | async-start | bytes 2621440 | tf_op jit(solution)/shard_map/all_to_all | solution.py:561
  24.4 1.0 broadcast_in_dim_reshape.8.bias
  25.5 3.8 %multiply_convert_fusion = bf16[128,8,20,8]{1,0,3,2:T(8,128)(2,1)} fusion(f32[8,8]{0,1:T(8,128)S(1)} %copy.36, f32[128,20]{0,1:T(8,128)S(1)} %fusion.13), kind=kLoop, calls=%fused_computation | loop fusion | flops 327680 | bytes 338176 | tf_op jit(solution)/shard_map/convert_element_type | solution.py:580
  29.3 8.5 %convert_element_type.54 = bf16[1024,160]{0,1:T(8,128)(2,1)S(1)} reshape(bf16[128,8,20,8]{1,0,3,2:T(8,128)(2,1)} %multiply_convert_fusion) | data formatting | bytes 655360 | tf_op jit(solution)/shard_map/convert_element_type | solution.py:580
  37.8 1.0 copy.37.skip
  38.8 2.8 %broadcast_multiply_fusion = bf16[20,8,128,8]{3,2,1,0:T(8,128)(2,1)} fusion(bf16[8,8]{1,0:T(8,128)(2,1)S(1)} %fusion.8, bf16[20,128]{1,0:T(8,128)(2,1)S(1)} %bitcast.66), kind=kLoop, calls=%fused_computation.1 | loop fusion | flops 163840 | bytes 332928 | tf_op jit(solution)/shard_map/mul | solution.py:582
  41.6 9.1 %mul.58.closing = bf16[160,1024]{1,0:T(8,128)(2,1)} reshape(bf16[20,8,128,8]{3,2,1,0:T(8,128)(2,1)} %broadcast_multiply_fusion) | data formatting | bytes 655360 | tf_op jit(solution)/shard_map/mul | solution.py:582
  50.7 1.6 dynamic-slice_bitcast_fusion.back
  52.3 0.9 broadcast_multiply_fusion.1.bias_modes_row
  53.2 2.0 %copy.46 = bf16[1,4,1024,128]{3,1,2,0:T(4,128)(2,1)S(1)} copy(bf16[1,4,1024,128]{3,2,1,0:T(8,128)(2,1)} %bitcast.62) | data formatting | bytes 2097152
  55.8 0.8 copy.35
  56.6 1.5 reshape.65.first
  59.1 0.8 reshape.63.inner
  59.9 1.1 copy-done.1
  60.9 26.8 %mix.1.mixed = bf16[128,16,256]{2,1,0:T(8,128)(2,1)} custom-call(bf16[8,32,2560]{2,1,0:T(8,128)(2,1)} %copy-done.1, bf16[256,2048]{1,0:T(8,128)(2,1)} %constant.45.clone.height, bf16[2,320,1024]{2,1,0:T(8,128)(2,1)} %constant.41.clone.place, f32[128,1024]{1,0:T(8,128)} %broadcast_multiply_fusion.1.bias_modes_row, bf16[32,768]{1,0:T(8,128)(2,1)} %reshape.63.inner, ...), custom_call_target="tpu_custom_call" | custom-call | tf_op jit(solution)/shard_map/mix/pallas_call | solution.py:308
  87.7 87.7 %finish.1 = bf16[20,128,1024]{2,1,0:T(8,128)(2,1)} custom-call(bf16[128,16,256]{2,1,0:T(8,128)(2,1)} %mix.1.mixed, bf16[256,256]{1,0:T(8,128)(2,1)} %dynamic-slice_bitcast_fusion.back, bf16[20,128,1024]{2,1,0:T(8,128)(2,1)} %bitcast.55, bf16[256,1024]{1,0:T(8,128)(2,1)} %constant.39.clone.width, bf16[1024,160]{1,0:T(8,128)(2,1)} %copy.37.skip, ...), custom_call_target="tpu_custom_call" | custom-call | tf_op jit(solution)/shard_map/finish/pallas_call | solution.py:473
  175.4 5.7 %copy.49 = bf16[1,20,128,1024]{3,2,1,0:T(8,128)(2,1)} copy(bf16[1,20,128,1024]{3,2,1,0:T(8,128)(2,1)} %bitcast.54) | data formatting | bytes 10485760
  (37 shorter events, 3.3 us)
Async XLA Ops:
  6.5 17.6 %copy-start = (bf16[128,128]{1,0:T(8,128)(2,1)S(1)}, bf16[128,128]{1,0:T(8,128)(2,1)}, u32[]{:S(2)}) copy-start(bf16[128,128]{1,0:T(8,128)(2,1)} %param.26) | copy-start | bytes 98308
  6.5 46.6 %all-gather.2.cloned.1.call-start = ((), (), s32[]{:S(2)}) async-start(), calls=%async_computation.1 | async-start | bytes 1310720 | tf_op jit(solution)/shard_map/all_gather | solution.py:500
  15.5 7.8 %copy-start.5 = (f32[20]{0:T(128)S(1)}, f32[20]{0:T(128)}, u32[]{:S(2)}) copy-start(f32[20]{0:T(128)} %param.29) | copy-start | bytes 244
  15.6 8.6 %copy-start.6 = (f32[128]{0:T(128)S(1)}, f32[128]{0:T(128)}, u32[]{:S(2)}) copy-start(f32[128]{0:T(128)} %param.27) | copy-start | bytes 1540
  15.6 8.6 %copy-start.7 = (f32[128]{0:T(128)S(1)}, f32[128]{0:T(128)}, u32[]{:S(2)}) copy-start(f32[128]{0:T(128)} %param.21) | copy-start | bytes 1540
  15.6 9.8 %copy-start.4 = (bf16[20,128]{1,0:T(8,128)(2,1)S(1)}, bf16[20,128]{1,0:T(8,128)(2,1)}, u32[]{:S(2)}) copy-start(bf16[20,128]{1,0:T(8,128)(2,1)} %param.20) | copy-start | bytes 15364
  18.1 41.8 %all-to-all-start = ((bf16[8,32,2560]{2,1,0:T(8,128)(2,1)}), bf16[8,32,2560]{2,1,0:T(8,128)(2,1)S(1)}, u32[]{:S(2)}, u32[]{:S(2)}) async-start(bf16[8,32,2560]{2,1,0:T(8,128)(2,1)} %reshape.57), calls=%async_computation | async-start | bytes 2621440 | tf_op jit(solution)/shard_map/all_to_all | solution.py:561
  25.5 13.3 %copy-start.3 = (bf16[128,20]{0,1:T(8,128)(2,1)S(1)}, bf16[128,20]{0,1:T(8,128)(2,1)}, u32[]{:S(2)}) copy-start(bf16[128,20]{0,1:T(8,128)(2,1)} %param.28) | copy-start | bytes 15364
  38.8 13.5 %copy-start.2 = (f32[128,1024]{1,0:T(8,128)S(1)}, f32[128,1024]{1,0:T(8,128)}, u32[]{:S(2)}) copy-start(f32[128,1024]{1,0:T(8,128)} %constant.42.clone) | copy-start | bytes 1572868
  59.9 1.1 copy-start.1
Sparse Core Ops, SparseCore 0:
  11.4 30.6 all-gather.1

commit v2 on v1

--- a/solution.py
+++ b/solution.py
@@ -173,8 +173,11 @@
 WAVES = 16
 SLOTS = 32
 EIGHT = 8
-CHUNKS = 4
+CHUNKS = (64, 64)
+STARTS = (0, 64)
 LANES = 512
+ROWS = 256
+PARTS = 2
 
 
 def whole(a):
@@ -182,21 +185,165 @@
 
 
 def mix_kernel(
-    arrived, height, place, bias_modes_row, inner, second, first, first_spread, outer, spread,
-    mixed, stacked, placed, inner_wide, turned_inner, weights, rows, blocks, closing, carried, turned,
+    fields_far, forward, first_own, inner_own, outer_own, height, place, bias_row, second, first_spread, spread,
+    mixed, fields, modes, arrived, first, inner, outer, stacked, placed, inner_wide, turned_inner, weights, rows,
+    blocks, closing, carried, turned, load, send_plane, recv_plane, send_near, recv_near, send_modes, recv_modes,
 ):
+    variables, row_count, points = fields.shape
     holders, lead, flat = arrived.shape
     waves = lead // 2
-    variables = stacked.shape[0] // waves
-    row_count = flat // variables
     kx_count = height.shape[0] // 2
-    rank = first.shape[1]
-    channels = outer.shape[0] // 2
+    planes = first.shape[0]
+    rank = inner.shape[1]
+    channels = mixed.shape[0]
     pairs = waves // 2
     wide = 4 * rank
-    slots = inner.shape[1] // rank
+    slots = inner.shape[2] // rank
     packs = kx_count // EIGHT
-
+    share = variables // PARTS
+    mode, batch, core = lax.axis_index("mode"), lax.axis_index("batch"), lax.axis_index("cores")
+    me = mode * 2 + core
+    near = (mode + 1 - 2 * (mode % 2), batch, core)
+
+    def load_part(c):
+        here = pl.ds(c * share, share)
+        return pltpu.make_async_copy(fields_far.at[here], fields.at[here], load.at[c])
+
+    for c in range(PARTS):
+        load_part(c).start()
+
+    def flip(bit, change):
+        return bit + change - 2 * bit * change
+
+    def peer(t):
+        chip, side, line = flip(mode // 2, t // 4), flip(mode % 2, t // 2 % 2), flip(core, t % 2)
+        return (chip * 2 + side, batch, line), chip * 4 + side * 2 + line
+
+    def plane(step):
+        return (mode, (batch + step) % planes, core)
+
+    barrier = pltpu.get_barrier_semaphore()
+    greeted = [peer(t)[0] for t in range(1, holders)] + [plane(step) for step in range(1, planes)]
+    for device in greeted:
+        pl.semaphore_signal(barrier, inc=1, device_id=device, device_id_type=MESH)
+    pl.semaphore_wait(barrier, len(greeted))
+
+    shards_own = (first_own, inner_own, outer_own)
+    shards_all = (first, inner, outer)
+
+    def half(n):
+        size = shards_own[n].shape[0] // 2
+        return pl.ds(pl.multiple_of((mode % 2) * size, size), size)
+
+    def plane_copy(step, n):
+        return pltpu.make_async_remote_copy(
+            src_ref=shards_own[n].at[half(n)], dst_ref=shards_all[n].at[batch, half(n)],
+            send_sem=send_plane.at[step - 1, n], recv_sem=recv_plane.at[step - 1, n],
+            device_id=plane(step), device_id_type=MESH,
+        )
+
+    def near_copy(step, n):
+        held = shards_all[n].at[(batch + planes - step) % planes, half(n)]
+        return pltpu.make_async_remote_copy(
+            src_ref=held, dst_ref=held, send_sem=send_near.at[step - 1, n], recv_sem=recv_near.at[step - 1, n],
+            device_id=near, device_id_type=MESH,
+        )
+
+    def modes_copy(t, c):
+        device, index = peer(t)
+        lanes = pl.ds(c * share * row_count, share * row_count)
+        return pltpu.make_async_remote_copy(
+            src_ref=modes.at[index, :, lanes], dst_ref=arrived.at[me, :, lanes],
+            send_sem=send_modes.at[t - 1, c], recv_sem=recv_modes.at[t - 1, c],
+            device_id=device, device_id_type=MESH,
+        )
+
+    for n in range(3):
+        for step in range(1, planes):
+            plane_copy(step, n).start()
+    for n in range(3):
+        shards_all[n][batch] = shards_own[n][...]
+
+    for c in range(PARTS):
+        load_part(c).wait()
+        for v in range(c * share, (c + 1) * share, 2):
+            both = fields[v:v + 2].reshape(2 * row_count, points)
+            got = dense(forward[...], both, ((1,), (1,))).astype(jnp.bfloat16)
+            modes[:, :, v * row_count:(v + 2) * row_count] = got.reshape(holders, lead, 2 * row_count)
+        for t in range(holders - 1, 0, -1):
+            modes_copy(t, c).start()
+    arrived[me] = modes[me]
+
+    for n in range(2):
+        for step in range(1, planes):
+            plane_copy(step, n).wait_recv()
+            near_copy(step, n).start()
+    for n in range(2):
+        for step in range(1, planes):
+            near_copy(step, n).wait_recv()
+
+    total = inner[0].astype(jnp.float32)
+    for z in range(1, planes):
+        total = total + inner[z].astype(jnp.float32)
+    total = total.astype(jnp.bfloat16)
+    for part in range(slots // 4):
+        inner_wide[:, part * 4 * wide:(part + 1) * 4 * wide] = dense(
+            total[:, part * wide:(part + 1) * wide], spread[:wide, :4 * wide]
+        ).astype(jnp.bfloat16)
+
+    down = lax.broadcasted_iota(jnp.int32, (rank * EIGHT, rank * EIGHT), 0) % EIGHT
+    along = lax.broadcasted_iota(jnp.int32, (rank * EIGHT, rank * EIGHT), 1) % EIGHT
+    same = down == along
+    for z in range(planes):
+        for k in range(packs // planes):
+            full = dense(first[z], first_spread[k])
+            blocks[z * (packs // planes) + k] = jnp.where(same, full, 0.0).astype(jnp.bfloat16)
+
+    turned_inner[...] = jnp.zeros_like(turned_inner)
+    group_of = lax.broadcasted_iota(jnp.int32, (SLOTS, wide), 1) // rank
+
+    def weight_step(j, carry):
+        start = pl.multiple_of(j * 2 * rank, 2 * rank)
+        joined = dense(second[pl.ds(start, 2 * rank), :], inner_wide[...])
+        for m in range(2):
+            for v in range(slots):
+                turned_inner[m, :, v, :] = joined[m * rank:(m + 1) * rank, v * wide:(v + 1) * wide]
+        for m in range(2):
+            for b in range(rank):
+                value = turned_inner[m, b]
+                for q in range(2):
+                    weights[j, (q * 2 + m) * SLOTS:(q * 2 + m + 1) * SLOTS, b * wide:(b + 1) * wide] = jnp.where(
+                        group_of == m * 2 + q, value, 0.0
+                    ).astype(jnp.bfloat16)
+        return carry
+
+    lax.fori_loop(0, pairs, weight_step, 0)
+
+    for step in range(1, planes):
+        plane_copy(step, 2).wait_recv()
+        near_copy(step, 2).start()
+    for step in range(1, planes):
+        near_copy(step, 2).wait_recv()
+    count = channels // planes
+    lanes = lax.broadcasted_iota(jnp.int32, (count, 8 * wide), 1)
+    part_of = lanes // rank % 2
+    wave_of = lanes // (2 * rank) % 2
+    for part in range(rank // 8):
+        for z in range(planes):
+            columns = slice(part * 8 * rank, (part + 1) * 8 * rank)
+            real = dense(outer[z, :count, columns], spread[...])
+            imaginary = dense(outer[z, count:, columns], spread[...])
+            for r in range(2):
+                value = jnp.where(part_of == 0, imaginary, real) if r else jnp.where(part_of == 0, real, -imaginary)
+                for m in range(2):
+                    start = (m * 2 + r) * channels + z * count
+                    closing[start:start + count, part * 8 * wide:(part + 1) * 8 * wide] = (
+                        jnp.where(wave_of == m, value, 0.0).astype(jnp.bfloat16)
+                    )
+
+    for c in range(PARTS):
+        for t in range(1, holders):
+            modes_copy(t, c).wait_recv()
     for d in range(holders):
         for p in range(2):
             for v in range(variables):
@@ -205,59 +352,14 @@
                 )
     by = dense(height[...], stacked[...], ((1,), (1,))).astype(jnp.bfloat16)
     placed[...] = (
-        dense(by[:kx_count], place[0]) + dense(by[kx_count:], place[1]) + bias_modes_row[...]
+        dense(by[:kx_count], place[0]) + dense(by[kx_count:], place[1]) + bias_row[...]
     ).astype(jnp.bfloat16)
 
-    for part in range(slots // 4):
-        inner_wide[:, part * 4 * wide:(part + 1) * 4 * wide] = dense(
-            inner[:, part * wide:(part + 1) * wide], spread[:wide, :4 * wide]
-        ).astype(jnp.bfloat16)
-
-    down = lax.broadcasted_iota(jnp.int32, (rank * EIGHT, rank * EIGHT), 0) % EIGHT
-    across = lax.broadcasted_iota(jnp.int32, (rank * EIGHT, rank * EIGHT), 1) % EIGHT
-    same = down == across
-
-    def block_step(k, carry):
-        start = pl.multiple_of(k * rank * EIGHT, rank * EIGHT)
-        full = dense(first[pl.ds(start, rank * EIGHT), :], first_spread[...])
-        blocks[k] = jnp.where(same, full, 0.0).astype(jnp.bfloat16)
-        return carry
-
-    lax.fori_loop(0, packs, block_step, 0)
-
-    lanes = lax.broadcasted_iota(jnp.int32, (channels, 8 * wide), 1)
-    part_of = lanes // rank % 2
-    wave_of = lanes // (2 * rank) % 2
-    for part in range(rank // 8):
-        real = dense(outer[:channels, part * 8 * rank:(part + 1) * 8 * rank], spread[...])
-        imaginary = dense(outer[channels:, part * 8 * rank:(part + 1) * 8 * rank], spread[...])
-        for r in range(2):
-            value = jnp.where(part_of == 0, imaginary, real) if r else jnp.where(part_of == 0, real, -imaginary)
-            for m in range(2):
-                closing[(m * 2 + r) * channels:(m * 2 + r + 1) * channels, part * 8 * wide:(part + 1) * 8 * wide] = (
-                    jnp.where(wave_of == m, value, 0.0).astype(jnp.bfloat16)
-                )
-
-    turned_inner[...] = jnp.zeros_like(turned_inner)
-    group_of = lax.broadcasted_iota(jnp.int32, (SLOTS, wide), 1) // rank
-
     def pair_step(j, carry):
-        start = pl.multiple_of(j * 2 * rank, 2 * rank)
         column = pl.ds(pl.multiple_of(j * wide, wide), wide)
-        joined = dense(second[pl.ds(start, 2 * rank), :], inner_wide[...])
-        for m in range(2):
-            for v in range(slots):
-                turned_inner[m, :, v, :] = joined[m * rank:(m + 1) * rank, v * wide:(v + 1) * wide]
-        for m in range(2):
-            for b in range(rank):
-                value = turned_inner[m, b]
-                for q in range(2):
-                    weights[(q * 2 + m) * SLOTS:(q * 2 + m + 1) * SLOTS, b * wide:(b + 1) * wide] = jnp.where(
-                        group_of == m * 2 + q, value, 0.0
-                    ).astype(jnp.bfloat16)
         own = placed[:, column]
         for part in range(rank // 8):
-            got = dense(own, weights[:, part * 8 * wide:(part + 1) * 8 * wide])
+            got = dense(own, weights[j, :, part * 8 * wide:(part + 1) * 8 * wide])
             for k in range(packs):
                 rows[k, part * 64:(part + 1) * 64, column] = jnp.concatenate(
                     [got[k * EIGHT:(k + 1) * EIGHT, b * wide:(b + 1) * wide] for b in range(8)], axis=0
@@ -294,35 +396,60 @@
                     ]
     mixed[...] = turned[...].astype(jnp.bfloat16)
 
-
-def mix(arrived, height, place, bias_row, inner, second, first, first_spread, outer, spread):
-    holders, lead, flat = arrived.shape
-    waves = lead // 2
+    for n in range(3):
+        for step in range(1, planes):
+            plane_copy(step, n).wait_send()
+            near_copy(step, n).wait_send()
+    for c in range(PARTS):
+        for t in range(1, holders):
+            modes_copy(t, c).wait_send()
+
+
+def mix(fields, forward, first, inner, outer, height, place, bias_row, second, first_spread, spread, planes):
+    variables, row_count, points = fields.shape
+    holders = forward.shape[0] // (2 * WAVES)
+    waves = WAVES
     kx2, depth = height.shape
-    rank = first.shape[1]
-    channels = outer.shape[0] // 2
+    rank = inner.shape[0]
+    channels = outer.shape[0] // 2 * planes
     wide = 4 * rank
     slots = inner.shape[1] // rank
     packs = kx2 // 2 // EIGHT
-    operands = (arrived, height, place, bias_row, inner, second, first, first_spread, outer, spread)
+    operands = (fields, forward, first, inner, outer, height, place, bias_row, second, first_spread, spread)
     return pl.pallas_call(
         mix_kernel,
-        in_specs=[pl.BlockSpec(memory_space=pltpu.VMEM) for _ in operands],
+        in_specs=[pl.BlockSpec(memory_space=pl.ANY)]
+        + [pl.BlockSpec(memory_space=pltpu.VMEM) for _ in operands[1:]],
         out_specs=pl.BlockSpec(memory_space=pltpu.VMEM),
         out_shape=jax.ShapeDtypeStruct((channels, waves, kx2), jnp.bfloat16),
         scratch_shapes=[
+            pltpu.VMEM(fields.shape, jnp.bfloat16),
+            pltpu.VMEM((holders, 2 * waves, variables * row_count), jnp.bfloat16),
+            pltpu.VMEM((holders, 2 * waves, variables * row_count), jnp.bfloat16),
+            pltpu.VMEM((planes,) + first.shape, jnp.bfloat16),
+            pltpu.VMEM((planes,) + inner.shape, jnp.bfloat16),
+            pltpu.VMEM((planes,) + outer.shape, jnp.bfloat16),
             pltpu.VMEM((place.shape[1], depth), jnp.bfloat16),
             pltpu.VMEM((kx2 // 2, waves // 2 * wide), jnp.bfloat16),
             pltpu.VMEM((rank, slots * wide), jnp.bfloat16),
             pltpu.VMEM((2, rank, SLOTS, wide), jnp.float32),
-            pltpu.VMEM((4 * SLOTS, rank * wide), jnp.bfloat16),
+            pltpu.VMEM((waves // 2, 4 * SLOTS, rank * wide), jnp.bfloat16),
             pltpu.VMEM((packs, rank * EIGHT, waves // 2 * wide), jnp.bfloat16),
             pltpu.VMEM((packs, rank * EIGHT, rank * EIGHT), jnp.bfloat16),
             pltpu.VMEM((4 * channels, rank * wide), jnp.bfloat16),
             pltpu.VMEM((waves // 2, kx2 // 2, rank * wide), jnp.bfloat16),
             pltpu.VMEM((channels, waves, kx2), jnp.float32),
+            pltpu.SemaphoreType.DMA((PARTS,)),
+            pltpu.SemaphoreType.DMA((planes - 1, 3)),
+            pltpu.SemaphoreType.DMA((planes - 1, 3)),
+            pltpu.SemaphoreType.DMA((planes - 1, 3)),
+            pltpu.SemaphoreType.DMA((planes - 1, 3)),
+            pltpu.SemaphoreType.DMA((holders - 1, PARTS)),
+            pltpu.SemaphoreType.DMA((holders - 1, PARTS)),
         ],
-        compiler_params=pltpu.CompilerParams(vmem_limit_bytes=56 * 2**20),
+        compiler_params=pltpu.CompilerParams(
+            collective_id=1, has_side_effects=True, vmem_limit_bytes=60 * 2**20
+        ),
         name="mix",
     )(*operands)
 
@@ -332,14 +459,13 @@
 
 
 def finish_kernel(
-    mixed, back, fields, width, skip, bias, closing, out_bias,
-    result, gathered, source, cols, total, send, recv,
+    mixed, back, fields, width, lift_weight, skip_weight, lift_bias, skip_bias, out_weight, out_bias, tall, wide,
+    result, gathered, source, cols, total, skip, closing, last_bias, active, send, recv,
 ):
     channels, waves, kx2 = mixed.shape
     variables, row_count, points = fields.shape
-    share = channels // CHUNKS
-    depth = share * EIGHT
-    half = share // 2
+    inner = variables * EIGHT
+    steps = row_count // EIGHT // 2
     mode, batch, core = lax.axis_index("mode"), lax.axis_index("batch"), lax.axis_index("cores")
     near = (mode + 1 - 2 * (mode % 2), batch, core)
     by_x = ((mode + 2) % 4, batch, core)
@@ -361,7 +487,8 @@
         return gathered.at[pl.ds(first, count), pl.ds(pl.multiple_of(holder * waves, waves), waves), :]
 
     def copy(g, kind):
-        low = g * share
+        low, share = STARTS[g], CHUNKS[g]
+        half = share // 2
         own = mixed.at[pl.ds(low, share)]
         home = piece(me, low, share)
         x_all, y_all = piece(at_x, low, share), piece(at_y, low, share)
@@ -389,7 +516,7 @@
     def relay(g):
         came(g, (1, 2))
         begin(g, (5, 6, 3, 4))
-        if g + 1 < CHUNKS:
+        if g + 1 < len(CHUNKS):
             begin(g + 1, (1, 2, 0))
 
     def relay_last(g):
@@ -398,31 +525,63 @@
 
     begin(0, (1, 2, 0))
     gathered[:, pl.ds(pl.multiple_of(me * waves, waves), waves), :] = mixed[...]
-    for x in range(row_count // EIGHT // 2):
+
+    depth = skip.shape[1]
+    line = lax.broadcasted_iota(jnp.int32, (depth - inner, points), 0)
+    ones = jnp.where(line < 2, 1.0, 0.0).astype(jnp.bfloat16)
+    for x in range(steps):
         rows = fields[:, x * 2 * EIGHT:(x + 1) * 2 * EIGHT, :]
         for h in range(2):
-            source[x * 2 + h] = rows[:, h * EIGHT:(h + 1) * EIGHT, :].reshape(variables * EIGHT, points)
+            source[x * 2 + h, :inner, :] = rows[:, h * EIGHT:(h + 1) * EIGHT, :].reshape(inner, points)
+            source[x * 2 + h, inner:, :] = ones
     relay(0)
+
+    direct = dense(lift_weight[...], skip_weight[...]).astype(jnp.bfloat16)
+    row_bias = lax.dot_general(
+        jnp.broadcast_to(lift_bias[...], (8, channels)), skip_weight[...].astype(jnp.float32),
+        (((1,), (0,)), ((), ())), preferred_element_type=jnp.float32, precision=lax.Precision.HIGHEST,
+    )[:1] + skip_bias[...]
+    size = 256
+    down = lax.broadcasted_iota(jnp.int32, (size, depth), 0) % EIGHT
+    along = lax.broadcasted_iota(jnp.int32, (size, depth), 1)
+    for part in range(channels * EIGHT // size):
+        here = slice(part * size, (part + 1) * size)
+        picked = dense(tall[here, :], direct, ((1,), (1,))).astype(jnp.bfloat16)
+        spread = dense(picked, wide[:variables, :depth])
+        column = jnp.sum(tall[here, :].astype(jnp.float32) * row_bias, axis=1, keepdims=True)
+        high = column.astype(jnp.bfloat16).astype(jnp.float32)
+        rest = jnp.where(along == inner, high, jnp.where(along == inner + 1, column - high, 0.0))
+        skip[here, :] = jnp.where(
+            along < inner, jnp.where(down == along % EIGHT, spread, 0.0), rest
+        ).astype(jnp.bfloat16)
+    chosen = dense(tall[:inner, :variables], out_weight[...], ((1,), (1,))).astype(jnp.bfloat16)
+    down = lax.broadcasted_iota(jnp.int32, (inner, channels * EIGHT), 0) % EIGHT
+    along = lax.broadcasted_iota(jnp.int32, (inner, channels * EIGHT), 1) % EIGHT
+    closing[...] = jnp.where(down == along, dense(chosen, wide[...]), 0.0).astype(jnp.bfloat16)
+    column = jnp.sum(tall[:inner, :variables].astype(jnp.float32) * out_bias[...], axis=1, keepdims=True)
+    last_bias[...] = jnp.broadcast_to(column, last_bias.shape)
     relay_last(0)
 
     def turn(g):
         def step(c, carry):
-            both = gathered[pl.ds(g * share + 2 * c, 2)].reshape(2 * waves * 8, kx2)
+            both = gathered[pl.ds(STARTS[g] + 4 * c, 4)].reshape(4 * waves * 8, kx2)
             got = dense(back[...], both, ((1,), (1,)))
-            place = pl.ds(pl.multiple_of(c * 2 * EIGHT, 2 * EIGHT), 2 * EIGHT)
-            size = got.shape[1] // 2
-            for p in range(2):
-                for x in range(row_count // EIGHT):
-                    rows = got[p * row_count + x * EIGHT:p * row_count + (x + 1) * EIGHT, :]
-                    cols[x, place, p * size:(p + 1) * size] = jnp.concatenate(
-                        [rows[:, :size], rows[:, size:]], axis=0
-                    ).astype(jnp.bfloat16)
+            size = got.shape[1] // 4
+            for k in range(2):
+                place = pl.ds(pl.multiple_of(c * 4 * EIGHT + k * 2 * EIGHT, 2 * EIGHT), 2 * EIGHT)
+                for p in range(2):
+                    for x in range(row_count // EIGHT):
+                        rows = got[p * row_count + x * EIGHT:p * row_count + (x + 1) * EIGHT, :]
+                        cols[x, place, p * size:(p + 1) * size] = jnp.concatenate(
+                            [rows[:, 2 * k * size:(2 * k + 1) * size], rows[:, (2 * k + 1) * size:(2 * k + 2) * size]],
+                            axis=0,
+                        ).astype(jnp.bfloat16)
             return carry
 
-        lax.fori_loop(0, share // 2, step, 0)
+        lax.fori_loop(0, CHUNKS[g] // 4, step, 0)
 
     def finish_rows(g, low, high):
-        part = slice(g * depth, (g + 1) * depth)
+        start, size = STARTS[g] * EIGHT, CHUNKS[g] * EIGHT
 
         def step(i, carry):
             for lane in range(points // LANES):
@@ -430,13 +589,20 @@
                 done = []
                 for h in range(2):
                     x = 2 * i + h
-                    height = (
-                        dense(cols[x], width[:, lanes]) + dense(skip[part, :], source[x, :, lanes]) + bias[part, :]
-                    )
-                    active = gelu(height).astype(jnp.bfloat16)
-                    got = dense(closing[:, part], active)
-                    got = got + (out_bias[...] if g == 0 else total[x, :, lanes])
-                    if g + 1 < CHUNKS:
+                    for part in range(0, size, ROWS):
+                        height = (
+                            dense(cols[x, part:part + ROWS, :], width[:, lanes])
+                            + dense(skip[start + part:start + part + ROWS, :], source[x, :, lanes])
+                        )
+                        active[lane * 2 + h, part:part + ROWS, :] = gelu(height).astype(jnp.bfloat16)
+                for h in range(2):
+                    x = 2 * i + h
+                    got = dense(closing[:, start:start + size], active[lane * 2 + h, :size, :])
+                    if g == 0:
+                        got = got + jnp.concatenate([last_bias[...]] * (LANES // 128), axis=1)
+                    else:
+                        got = got + total[x, :, lanes]
+                    if g + 1 < len(CHUNKS):
                         total[x, :, lanes] = got
                     else:
                         done.append(got.reshape(variables, EIGHT, LANES))
@@ -447,29 +613,34 @@
 
         lax.fori_loop(low, high, step, 0)
 
-    steps = row_count // EIGHT // 2
-    for g in range(CHUNKS):
+    for g in range(len(CHUNKS)):
         came(g, (0, 3, 4, 7, 8))
         turn(g)
-        if g + 1 < CHUNKS:
+        if g + 1 < len(CHUNKS):
             finish_rows(g, 0, steps // 4)
             relay(g + 1)
-            finish_rows(g, steps // 4, 5 * steps // 8)
+            finish_rows(g, steps // 4, 3 * steps // 4)
             relay_last(g + 1)
-            finish_rows(g, 5 * steps // 8, steps)
+            finish_rows(g, 3 * steps // 4, steps)
         else:
             finish_rows(g, 0, steps)
-    for g in range(CHUNKS):
+    for g in range(len(CHUNKS)):
         for kind in range(9):
             copy(g, kind).wait_send()
 
 
-def finish(mixed, back, fields, width, skip, bias, closing, out_bias):
+def finish(mixed, back, fields, width, lift_weight, skip_weight, lift_bias, skip_bias, out_weight, out_bias):
     channels, waves, kx2 = mixed.shape
     variables, row_count, points = fields.shape
-    operands = (mixed, back, fields, width, skip, bias, closing, out_bias)
-    share = channels // CHUNKS
+    tall = jnp.asarray(np.repeat(np.eye(channels), EIGHT, axis=0).astype(ml_dtypes.bfloat16))
+    wide = jnp.asarray(np.repeat(np.eye(channels), EIGHT, axis=1).astype(ml_dtypes.bfloat16))
+    operands = (
+        mixed, back, fields, width, lift_weight, skip_weight, lift_bias[None], skip_bias[None], out_weight,
+        out_bias[None], tall, wide,
+    )
     blocks = row_count // EIGHT
+    inner = variables * EIGHT
+    depth = inner + 2 * EIGHT
     return pl.pallas_call(
         finish_kernel,
         in_specs=[pl.BlockSpec(memory_space=pltpu.VMEM) for _ in operands],
@@ -477,34 +648,21 @@
         out_shape=jax.ShapeDtypeStruct(fields.shape, jnp.bfloat16),
         scratch_shapes=[
             pltpu.VMEM((channels, 8 * waves, kx2), jnp.bfloat16),
-            pltpu.VMEM((blocks, variables * EIGHT, points), jnp.bfloat16),
-            pltpu.VMEM((blocks, share * EIGHT, width.shape[0]), jnp.bfloat16),
-            pltpu.VMEM((blocks, variables * EIGHT, points), jnp.float32),
-            pltpu.SemaphoreType.DMA((CHUNKS, 9)),
-            pltpu.SemaphoreType.DMA((CHUNKS, 9)),
+            pltpu.VMEM((blocks, depth, points), jnp.bfloat16),
+            pltpu.VMEM((blocks, max(CHUNKS) * EIGHT, width.shape[0]), jnp.bfloat16),
+            pltpu.VMEM((blocks, inner, points), jnp.float32),
+            pltpu.VMEM((channels * EIGHT, depth), jnp.bfloat16),
+            pltpu.VMEM((inner, channels * EIGHT), jnp.bfloat16),
+            pltpu.VMEM((inner, 128), jnp.float32),
+            pltpu.VMEM((points // LANES * 2, max(CHUNKS) * EIGHT, LANES), jnp.bfloat16),
+            pltpu.SemaphoreType.DMA((len(CHUNKS), 9)),
+            pltpu.SemaphoreType.DMA((len(CHUNKS), 9)),
         ],
         compiler_params=pltpu.CompilerParams(
             collective_id=0, has_side_effects=True, vmem_limit_bytes=60 * 2**20
         ),
         name="finish",
     )(*operands)
-
-
-def gather_factors(first_core, input_core, output_core):
-    count, rank, _ = first_core.shape
-    first_core = first_core.reshape(count // EIGHT, EIGHT, rank, rank).transpose(0, 2, 1, 3)
-    output_core = output_core.transpose(1, 0, 3, 2)
-    flat = jnp.concatenate(
-        [first_core.reshape(-1), input_core.reshape(-1), output_core.reshape(-1)]
-    ).reshape(-1, 128)
-    gathered = lax.all_gather(flat, "batch", axis=0, tiled=False)
-    parts = gathered.shape[0]
-    size = first_core.size
-    gathered = gathered.reshape(parts, -1)
-    first = gathered[:, :size].reshape(-1, rank)
-    inner = gathered[:, size:2 * size].reshape(parts * count, rank * rank)
-    outer = gathered[:, 2 * size:].reshape(parts, 2, count, rank * rank).transpose(1, 0, 2, 3)
-    return first, inner, outer.reshape(2 * parts * count, rank * rank)
 
 
 def fast_shards(
@@ -549,41 +707,30 @@
     bias_row = np.zeros((MX, pairs, 2, 2, SLOTS), np.float32)
     bias_row[:, 0, :, 0, variables] = row_sum.reshape(2, MX).T
     bias_row = jnp.asarray(bias_row.reshape(MX, -1)) * (me == 0).astype(jnp.float32)
-    first_spread = jnp.asarray(np.repeat(np.eye(rank), EIGHT, axis=1).astype(ml_dtypes.bfloat16))
+    packs = first_core.shape[0] // EIGHT
+    first_spread = np.einsum("pk,bc->kpbc", np.eye(packs), np.repeat(np.eye(rank), EIGHT, axis=1))
+    first_spread = jnp.asarray(first_spread.reshape(packs, packs * rank, rank * EIGHT).astype(ml_dtypes.bfloat16))
     spread = np.eye(8)[:, None, :, None, None] * np.eye(rank)[None, :, None, None, :] * np.ones((1, 1, 1, 4, 1))
     spread = jnp.asarray(spread.reshape(8 * rank, 32 * rank).astype(ml_dtypes.bfloat16))
-
-    first, inner, outer = gather_factors(first_core, input_core, output_core)
-    modes = jnp.einsum(
-        "ry,vxy->rvx", forward, fields, preferred_element_type=jnp.float32
-    ).astype(jnp.bfloat16)
-    modes = modes.reshape(holders, 2 * waves, variables * row_count)
-    arrived = lax.all_to_all(modes, ("mode", "cores"), split_axis=0, concat_axis=0, tiled=True)
 
     used = (variables + 4) // 4 * 4
     lift = jnp.concatenate(
         [lift_weight, (math.sqrt(points) * lift_bias).astype(jnp.bfloat16)[None],
          jnp.zeros((used - variables - 1, channels), jnp.bfloat16)], 0
     )
-    inner = jnp.einsum(
-        "vc,cde->dve", lift, inner.reshape(channels, rank, rank), preferred_element_type=jnp.float32
-    ).astype(jnp.bfloat16).reshape(rank, used * rank)
+    count = input_core.shape[0]
+    lift = lax.dynamic_slice_in_dim(lift, lax.axis_index("batch") * count, count, 1)
+    inner = jnp.einsum("vc,cde->dve", lift, input_core, preferred_element_type=jnp.float32)
+    inner = inner.astype(jnp.bfloat16).reshape(rank, used * rank)
+    first = first_core.reshape(packs, EIGHT, rank, rank).transpose(2, 1, 0, 3).reshape(rank * EIGHT, packs * rank)
+    outer = output_core.transpose(1, 0, 3, 2).reshape(2 * count, rank * rank)
     mixed = mix(
-        arrived, jnp.asarray(height), place, bias_row, inner, second_core.reshape(waves * rank, rank),
-        first, first_spread, outer, spread,
-    )
-
-    skip_wide = skip_weight.astype(jnp.float32)
-    direct = jnp.dot(lift_weight.astype(jnp.float32), skip_wide, precision="highest")
-    total_bias = jnp.dot(lift_bias, skip_wide, precision="highest") + skip_bias
-    rows_eye = jnp.eye(EIGHT, dtype=jnp.float32)
-    skip = (direct.T[:, None, :, None] * rows_eye[None, :, None, :]).astype(jnp.bfloat16)
-    skip = skip.reshape(channels * EIGHT, variables * EIGHT)
-    closing = out_weight.T[:, None, :, None] * rows_eye.astype(jnp.bfloat16)[None, :, None, :]
-    closing = closing.reshape(variables * EIGHT, channels * EIGHT)
-    bias = jnp.repeat(total_bias, EIGHT)[:, None]
-    last_bias = jnp.repeat(out_bias, EIGHT)[:, None]
-    return finish(mixed, back_rows, fields, width, skip, bias, closing, last_bias)[None]
+        fields, forward, first, inner, outer, jnp.asarray(height), place, bias_row,
+        second_core.reshape(waves * rank, rank), first_spread, spread, lax.axis_size("batch"),
+    )
+    return finish(
+        mixed, back_rows, fields, width, lift_weight, skip_weight, lift_bias, skip_bias, out_weight, out_bias
+    )[None]
 
 
 def solution(mesh):
@@ -602,7 +749,7 @@
     )
     fits = (
         mesh.shape["mode"] == 4 and mesh.shape["cores"] == 2 and MY // 8 == WAVES
-        and MX // mesh.shape["batch"] % EIGHT == 0 and NX // 8 == 128
+        and mesh.shape["batch"] == 4 and MX // 4 % EIGHT == 0 and NX // 8 == 128
     )
     return jax.shard_map(
         fast_shards if fits else shards,

time: 190 us -> 130 us (0.68)
  local copies, waits for them, and re-layouts: 41.7 us -> 13.9 us
  between operations: 13.5 us -> 0.04 us
  other arithmetic: 8.14 us -> 2.58 us
  starting transfers between devices: 5.17 us -> 0 us
  matrix products: 4.87 us -> 0.95 us
  Pallas kernels: 114 us -> 112 us
    pallas_call x1, Pallas kernels: 87.7 us -> 66.8 us  [finish(): pl.pallas_call(finish_kernel, in_specs=[pl.BlockSpec(memory_space=pltpu.V...]
    pallas_call x1, Pallas kernels: 26.8 us -> 45.4 us  [mix(): pl.pallas_call(mix_kernel, in_specs=[pl.BlockSpec(memory_space=pl.ANY)] +...]
    convert_element_type x4 -> x0, local copies, waits for them, and re-layouts: 10.4 us -> none  [the longest x2 9.48 us: fast_shards(): (direct.T[:, None, :, None] * rows_eye[None, :, None, :]).astype(jnp.bflo...]
    mul x1 -> x0, local copies, waits for them, and re-layouts: 9.1 us -> none  [fast_shards(): out_weight.T[:, None, :, None]]
    all_to_all x1 -> x0, starting transfers between devices: 5.17 us -> none  [fast_shards(): lax.all_to_all(modes, ('mode', 'cores'), split_axis=0, concat_axis=0, til...]
    dot_general x4 -> x1, matrix products: 4.87 us -> 0.95 us  [fast_shards(): jnp.einsum('vc,cde->dve', lift, input_core, preferred_element_type=jnp.fl...]
    convert_element_type x3 -> x0, other arithmetic: 3.77 us -> none  [the longest x1 3.76 us: fast_shards(): (direct.T[:, None, :, None] * rows_eye[None, :, None, :]).astype(jnp.bflo...]
    mul x1 -> x0, other arithmetic: 2.77 us -> none  [fast_shards(): out_weight.T[:, None, :, None]]
  transfers between devices with their start and end apart: 2 -> 0, of which waited for: 0 -> 0; matrix products, arithmetic and copies ran while one was open for 23% -> 0% of each run, Pallas kernels for 0% -> 0%
where the time goes in v2:
time: 130 us
  Pallas kernels  112 us (86%)
  local copies, waits for them, and re-layouts  13.9 us (11%)
  other arithmetic  2.58 us (2%)
    pallas_call x1, Pallas kernels, finish(): pl.pallas_call(finish_kernel, in_specs=[pl.BlockSpec(memory_space=pltpu.V...  66.8 us
    pallas_call x1, Pallas kernels, mix(): pl.pallas_call(mix_kernel, in_specs=[pl.BlockSpec(memory_space=pl.ANY)] +...  45.4 us
    unnamed x4, local copies, waits for them, and re-layouts  7.08 us

profile of v2, /device:TPU:0, one launch (start us, length us, event | category | flops | bytes accessed | tf_op | source)
XLA Modules:
  0.0 129.7 jit_solution(18346943483584925218)
XLA Ops:
  0.0 0.0 copy-start
  0.0 0.7 convert_bitcast_fusion
  0.7 0.1 pad.2.clone
  0.8 1.4 %copy.25.out_weight = bf16[128,20]{1,0:T(8,128)(2,1)} copy(bf16[128,20]{0,1:T(8,128)(2,1)} %param.30) | data formatting | bytes 10240 | tf_op args[9]
  2.2 1.6 %dynamic-slice_bitcast_fusion.back = bf16[256,256]{1,0:T(8,128)(2,1)} fusion(bf16[8,256,256]{2,1,0:T(8,128)(2,1)} %constant.50.clone, s32[]{:T(128)S(6)} %select_n.8), kind=kLoop, calls=%fused_computation.5 | loop fusion | bytes 262148 | tf_op jit(solution)/shard_map/jit(dynamic_index_in_dim)/squeeze | solution.py:699
  3.8 0.0 copy-done
  3.8 1.0 fusion
  4.7 0.8 reshape.17.inner_own
  5.5 1.2 copy.29
  6.7 0.8 reshape.16.first_own
  7.5 1.9 %broadcast_multiply_fusion.bias_row = f32[128,1024]{1,0:T(8,128)} fusion(f32[128,1024]{1,0:T(8,128)} %constant.52.clone, f32[]{:T(128)S(6)} %convert_element_type.19), kind=kLoop, calls=%fused_computation.4 | loop fusion | flops 131072 | bytes 1048580 | tf_op jit(solution)/shard_map/mul | solution.py:709
  9.3 1.3 %copy.24 = bf16[2,32,32,32]{3,2,1,0:T(8,128)(2,1)S(1)} copy(bf16[2,32,32,32]{2,3,0,1:T(8,128)(2,1)} %bitcast.26) | data formatting | bytes 262144 | tf_op jit(solution)/shard_map/transpose | solution.py:726
  10.6 1.2 reshape.18.outer_own
  11.8 45.4 %mix.1.mixed = bf16[128,16,256]{2,1,0:T(8,128)(2,1)} custom-call(bf16[20,128,1024]{2,1,0:T(8,128)(2,1)} %bitcast.22, bf16[256,1024]{1,0:T(8,128)(2,1)} %constant.59.forward, bf16[256,128]{1,0:T(8,128)(2,1)} %reshape.16.first_own, bf16[32,768]{1,0:T(8,128)(2,1)} %reshape.17.inner_own, bf16[64,1024]{1,0:T(8,128)(2,1)} %reshape.18.outer_own, ...), custom_call_target="tpu_custom_call" | custom-call | tf_op jit(solution)/shard_map/mix/pallas_call | solution.py:419
  57.2 66.8 %finish.1 = bf16[20,128,1024]{2,1,0:T(8,128)(2,1)} custom-call(bf16[128,16,256]{2,1,0:T(8,128)(2,1)} %mix.1.mixed, bf16[256,256]{1,0:T(8,128)(2,1)} %dynamic-slice_bitcast_fusion.back, bf16[20,128,1024]{2,1,0:T(8,128)(2,1)} %bitcast.23, bf16[256,1024]{1,0:T(8,128)(2,1)} %constant.49.clone.width, bf16[20,128]{1,0:T(8,128)(2,1)} %lift_weight.1, ...), custom_call_target="tpu_custom_call" | custom-call | tf_op jit(solution)/shard_map/finish/pallas_call | solution.py:644
  124.0 5.7 %copy.31 = bf16[1,20,128,1024]{3,2,1,0:T(8,128)(2,1)} copy(bf16[1,20,128,1024]{3,2,1,0:T(8,128)(2,1)} %bitcast.24) | data formatting | bytes 10485760
  (1 shorter events, 0.0 us)
Async XLA Ops:
  0.0 3.8 %copy-start = (bf16[32,32,32]{2,1,0:T(8,128)(2,1)S(1)}, bf16[32,32,32]{2,1,0:T(8,128)(2,1)}, u32[]{:S(2)}) copy-start(bf16[32,32,32]{2,1,0:T(8,128)(2,1)} %param.26) | copy-start | bytes 196612

commit v3 on v2

--- a/solution.py
+++ b/solution.py
@@ -178,6 +178,7 @@
 LANES = 512
 ROWS = 256
 PARTS = 2
+TURN = 8
 
 
 def whole(a):
@@ -185,8 +186,8 @@
 
 
 def mix_kernel(
-    fields_far, forward, first_own, inner_own, outer_own, height, place, bias_row, second, first_spread, spread,
-    mixed, fields, modes, arrived, first, inner, outer, stacked, placed, inner_wide, turned_inner, weights, rows,
+    fields_far, forward, first_own, inner_own, outer_own, height_far, place_far, bias_row, second, first_spread, spread,
+    mixed, fields, height, place, modes, arrived, first, inner, outer, stacked, placed, inner_wide, turned_inner, weights, rows,
     blocks, closing, carried, turned, load, send_plane, recv_plane, send_near, recv_near, send_modes, recv_modes,
 ):
     variables, row_count, points = fields.shape
@@ -209,8 +210,13 @@
         here = pl.ds(c * share, share)
         return pltpu.make_async_copy(fields_far.at[here], fields.at[here], load.at[c])
 
+    def load_table(n):
+        return pltpu.make_async_copy((height_far, place_far)[n], (height, place)[n], load.at[PARTS + n])
+
     for c in range(PARTS):
         load_part(c).start()
+    for n in range(2):
+        load_table(n).start()
 
     def flip(bit, change):
         return bit + change - 2 * bit * change
@@ -341,6 +347,8 @@
                         jnp.where(wave_of == m, value, 0.0).astype(jnp.bfloat16)
                     )
 
+    for n in range(2):
+        load_table(n).wait()
     for c in range(PARTS):
         for t in range(1, holders):
             modes_copy(t, c).wait_recv()
@@ -351,8 +359,9 @@
                     arrived[d, p * waves:(p + 1) * waves, v * row_count:(v + 1) * row_count]
                 )
     by = dense(height[...], stacked[...], ((1,), (1,))).astype(jnp.bfloat16)
+    first_wave = (me == 0).astype(jnp.float32)
     placed[...] = (
-        dense(by[:kx_count], place[0]) + dense(by[kx_count:], place[1]) + bias_row[...]
+        dense(by[:kx_count], place[0]) + dense(by[kx_count:], place[1]) + bias_row[...] * first_wave
     ).astype(jnp.bfloat16)
 
     def pair_step(j, carry):
@@ -418,12 +427,13 @@
     operands = (fields, forward, first, inner, outer, height, place, bias_row, second, first_spread, spread)
     return pl.pallas_call(
         mix_kernel,
-        in_specs=[pl.BlockSpec(memory_space=pl.ANY)]
-        + [pl.BlockSpec(memory_space=pltpu.VMEM) for _ in operands[1:]],
+        in_specs=[pl.BlockSpec(memory_space=pl.ANY if n in (0, 5, 6) else pltpu.VMEM) for n in range(len(operands))],
         out_specs=pl.BlockSpec(memory_space=pltpu.VMEM),
         out_shape=jax.ShapeDtypeStruct((channels, waves, kx2), jnp.bfloat16),
         scratch_shapes=[
             pltpu.VMEM(fields.shape, jnp.bfloat16),
+            pltpu.VMEM(height.shape, jnp.bfloat16),
+            pltpu.VMEM(place.shape, jnp.bfloat16),
             pltpu.VMEM((holders, 2 * waves, variables * row_count), jnp.bfloat16),
             pltpu.VMEM((holders, 2 * waves, variables * row_count), jnp.bfloat16),
             pltpu.VMEM((planes,) + first.shape, jnp.bfloat16),
@@ -439,7 +449,7 @@
             pltpu.VMEM((4 * channels, rank * wide), jnp.bfloat16),
             pltpu.VMEM((waves // 2, kx2 // 2, rank * wide), jnp.bfloat16),
             pltpu.VMEM((channels, waves, kx2), jnp.float32),
-            pltpu.SemaphoreType.DMA((PARTS,)),
+            pltpu.SemaphoreType.DMA((PARTS + 2,)),
             pltpu.SemaphoreType.DMA((planes - 1, 3)),
             pltpu.SemaphoreType.DMA((planes - 1, 3)),
             pltpu.SemaphoreType.DMA((planes - 1, 3)),
@@ -459,8 +469,8 @@
 
 
 def finish_kernel(
-    mixed, back, fields, width, lift_weight, skip_weight, lift_bias, skip_bias, out_weight, out_bias, tall, wide,
-    result, gathered, source, cols, total, skip, closing, last_bias, active, send, recv,
+    mixed, back_far, fields_far, width, lift_weight, skip_weight, lift_bias, skip_bias, out_weight, out_bias, tall, wide,
+    result_far, gathered, back, fields, source, cols, total, skip, closing, last_bias, active, load, leave, send, recv,
 ):
     channels, waves, kx2 = mixed.shape
     variables, row_count, points = fields.shape
@@ -524,11 +534,19 @@
         begin(g, (7, 8))
 
     begin(0, (1, 2, 0))
+    loads = [
+        pltpu.make_async_copy(fields_far, fields, load.at[0]),
+        pltpu.make_async_copy(back_far.at[me], back, load.at[1]),
+    ]
+    for one in loads:
+        one.start()
     gathered[:, pl.ds(pl.multiple_of(me * waves, waves), waves), :] = mixed[...]
 
     depth = skip.shape[1]
     line = lax.broadcasted_iota(jnp.int32, (depth - inner, points), 0)
     ones = jnp.where(line < 2, 1.0, 0.0).astype(jnp.bfloat16)
+    for one in loads:
+        one.wait()
     for x in range(steps):
         rows = fields[:, x * 2 * EIGHT:(x + 1) * 2 * EIGHT, :]
         for h in range(2):
@@ -554,7 +572,7 @@
         skip[here, :] = jnp.where(
             along < inner, jnp.where(down == along % EIGHT, spread, 0.0), rest
         ).astype(jnp.bfloat16)
-    chosen = dense(tall[:inner, :variables], out_weight[...], ((1,), (1,))).astype(jnp.bfloat16)
+    chosen = dense(tall[:inner, :variables], out_weight[...]).astype(jnp.bfloat16)
     down = lax.broadcasted_iota(jnp.int32, (inner, channels * EIGHT), 0) % EIGHT
     along = lax.broadcasted_iota(jnp.int32, (inner, channels * EIGHT), 1) % EIGHT
     closing[...] = jnp.where(down == along, dense(chosen, wide[...]), 0.0).astype(jnp.bfloat16)
@@ -564,11 +582,11 @@
 
     def turn(g):
         def step(c, carry):
-            both = gathered[pl.ds(STARTS[g] + 4 * c, 4)].reshape(4 * waves * 8, kx2)
+            both = gathered[pl.ds(STARTS[g] + TURN * c, TURN)].reshape(TURN * waves * 8, kx2)
             got = dense(back[...], both, ((1,), (1,)))
-            size = got.shape[1] // 4
-            for k in range(2):
-                place = pl.ds(pl.multiple_of(c * 4 * EIGHT + k * 2 * EIGHT, 2 * EIGHT), 2 * EIGHT)
+            size = got.shape[1] // TURN
+            for k in range(TURN // 2):
+                place = pl.ds(pl.multiple_of(c * TURN * EIGHT + k * 2 * EIGHT, 2 * EIGHT), 2 * EIGHT)
                 for p in range(2):
                     for x in range(row_count // EIGHT):
                         rows = got[p * row_count + x * EIGHT:p * row_count + (x + 1) * EIGHT, :]
@@ -578,7 +596,11 @@
                         ).astype(jnp.bfloat16)
             return carry
 
-        lax.fori_loop(0, CHUNKS[g] // 4, step, 0)
+        lax.fori_loop(0, CHUNKS[g] // TURN, step, 0)
+
+    def leave_rows(i):
+        place = pl.ds(pl.multiple_of(i * 2 * EIGHT, 2 * EIGHT), 2 * EIGHT)
+        return pltpu.make_async_copy(fields.at[:, place, :], result_far.at[:, place, :], leave.at[i])
 
     def finish_rows(g, low, high):
         start, size = STARTS[g] * EIGHT, CHUNKS[g] * EIGHT
@@ -608,7 +630,9 @@
                         done.append(got.reshape(variables, EIGHT, LANES))
                 if done:
                     place = pl.ds(pl.multiple_of(i * 2 * EIGHT, 2 * EIGHT), 2 * EIGHT)
-                    result[:, place, lanes] = jnp.concatenate(done, axis=1).astype(jnp.bfloat16)
+                    fields[:, place, lanes] = jnp.concatenate(done, axis=1).astype(jnp.bfloat16)
+            if g + 1 == len(CHUNKS):
+                leave_rows(i).start()
             return carry
 
         lax.fori_loop(low, high, step, 0)
@@ -628,6 +652,12 @@
         for kind in range(9):
             copy(g, kind).wait_send()
 
+    def leave_step(i, carry):
+        leave_rows(i).wait()
+        return carry
+
+    lax.fori_loop(0, steps, leave_step, 0)
+
 
 def finish(mixed, back, fields, width, lift_weight, skip_weight, lift_bias, skip_bias, out_weight, out_bias):
     channels, waves, kx2 = mixed.shape
@@ -643,11 +673,13 @@
     depth = inner + 2 * EIGHT
     return pl.pallas_call(
         finish_kernel,
-        in_specs=[pl.BlockSpec(memory_space=pltpu.VMEM) for _ in operands],
-        out_specs=pl.BlockSpec(memory_space=pltpu.VMEM),
+        in_specs=[pl.BlockSpec(memory_space=pl.ANY if n in (1, 2) else pltpu.VMEM) for n in range(len(operands))],
+        out_specs=pl.BlockSpec(memory_space=pl.ANY),
         out_shape=jax.ShapeDtypeStruct(fields.shape, jnp.bfloat16),
         scratch_shapes=[
             pltpu.VMEM((channels, 8 * waves, kx2), jnp.bfloat16),
+            pltpu.VMEM(back.shape[1:], jnp.bfloat16),
+            pltpu.VMEM(fields.shape, jnp.bfloat16),
             pltpu.VMEM((blocks, depth, points), jnp.bfloat16),
             pltpu.VMEM((blocks, max(CHUNKS) * EIGHT, width.shape[0]), jnp.bfloat16),
             pltpu.VMEM((blocks, inner, points), jnp.float32),
@@ -655,6 +687,8 @@
             pltpu.VMEM((inner, channels * EIGHT), jnp.bfloat16),
             pltpu.VMEM((inner, 128), jnp.float32),
             pltpu.VMEM((points // LANES * 2, max(CHUNKS) * EIGHT, LANES), jnp.bfloat16),
+            pltpu.SemaphoreType.DMA((2,)),
+            pltpu.SemaphoreType.DMA((blocks // 2,)),
             pltpu.SemaphoreType.DMA((len(CHUNKS), 9)),
             pltpu.SemaphoreType.DMA((len(CHUNKS), 9)),
         ],
@@ -674,12 +708,11 @@
     _, variables, row_count, points = fields.shape
     channels = lift_weight.shape[1]
     fields = fields[0]
-    me = lax.axis_index("mode") * lax.axis_size("cores") + lax.axis_index("cores")
 
     cosines, sines = host_pair(np.arange(MY), np.arange(points), points)
     root = math.sqrt(points)
     forward = np.stack([cosines, -sines], 0).reshape(2, holders, waves, points).transpose(1, 0, 2, 3)
-    forward = jnp.asarray((forward.reshape(2 * MY, points) / root).astype(np.float32)).astype(jnp.bfloat16)
+    forward = jnp.asarray((forward.reshape(2 * MY, points) / root).astype(np.float32).astype(ml_dtypes.bfloat16))
     weight = np.where(np.arange(MY) == 0, 1.0, 2.0).astype(np.float32)[:, None]
     width = np.concatenate([cosines * weight, -sines * weight], 0) / root
     width = jnp.asarray(width.astype(ml_dtypes.bfloat16))
@@ -696,7 +729,6 @@
     up = np.concatenate([cos_t, -sin_t], 2)
     low = np.concatenate([sin_t, cos_t], 2)
     back_rows = jnp.asarray(np.concatenate([up, low], 1).astype(ml_dtypes.bfloat16))
-    back_rows = lax.dynamic_index_in_dim(back_rows, me, 0, keepdims=False)
     pairs = waves // 2
     place = np.zeros((2, variables, waves, pairs, 2, 2, SLOTS), np.float32)
     for q in range(2):
@@ -706,7 +738,7 @@
     place = jnp.asarray(place.reshape(2, variables * waves, -1).astype(ml_dtypes.bfloat16))
     bias_row = np.zeros((MX, pairs, 2, 2, SLOTS), np.float32)
     bias_row[:, 0, :, 0, variables] = row_sum.reshape(2, MX).T
-    bias_row = jnp.asarray(bias_row.reshape(MX, -1)) * (me == 0).astype(jnp.float32)
+    bias_row = jnp.asarray(bias_row.reshape(MX, -1))
     packs = first_core.shape[0] // EIGHT
     first_spread = np.einsum("pk,bc->kpbc", np.eye(packs), np.repeat(np.eye(rank), EIGHT, axis=1))
     first_spread = jnp.asarray(first_spread.reshape(packs, packs * rank, rank * EIGHT).astype(ml_dtypes.bfloat16))
@@ -729,7 +761,7 @@
         second_core.reshape(waves * rank, rank), first_spread, spread, lax.axis_size("batch"),
     )
     return finish(
-        mixed, back_rows, fields, width, lift_weight, skip_weight, lift_bias, skip_bias, out_weight, out_bias
+        mixed, back_rows, fields, width, lift_weight, skip_weight, lift_bias, skip_bias, out_weight.T, out_bias
     )[None]
 
 

time: 130 us -> 120 us (0.923)
  Pallas kernels: 112 us -> 107 us
  local copies, waits for them, and re-layouts: 13.9 us -> 11.1 us
  other arithmetic: 2.58 us -> 0.7 us
    pallas_call x2, Pallas kernels: 112 us -> 107 us  [the longest x1 62.2 us: finish(): pl.pallas_call(finish_kernel, in_specs=[pl.BlockSpec(memory_space=pl.ANY...]
    mul x1 -> x0, other arithmetic: 1.88 us -> none  [fast_shards(): jnp.asarray(bias_row.reshape(MX, -1)) * (me == 0).astype(jnp.float32)]
    squeeze x1 -> x0, local copies, waits for them, and re-layouts: 1.56 us -> none  [fast_shards(): back_rows = lax.dynamic_index_in_dim(back_rows, me, 0, keepdims=False)]
    unnamed x4 -> x3, local copies, waits for them, and re-layouts: 7.08 us -> 5.84 us
where the time goes in v3:
time: 120 us
  Pallas kernels  107 us (89%)
  local copies, waits for them, and re-layouts  11.1 us (9%)
    pallas_call x1, Pallas kernels, finish(): pl.pallas_call(finish_kernel, in_specs=[pl.BlockSpec(memory_space=pl.ANY...  62.2 us
    pallas_call x1, Pallas kernels, mix(): pl.pallas_call(mix_kernel, in_specs=[pl.BlockSpec(memory_space=pl.ANY if...  44.7 us
    unnamed x3, local copies, waits for them, and re-layouts  5.84 us

profile of v3, /device:TPU:0, one launch (start us, length us, event | category | flops | bytes accessed | tf_op | source)
XLA Modules:
  0.0 119.7 jit_solution(16364990746571635860)
XLA Ops:
  0.0 0.0 copy-start
  0.0 0.7 convert_bitcast_fusion
  0.7 0.1 pad.2.clone
  0.8 0.2 copy-done
  1.0 1.0 fusion
  1.9 0.8 reshape.17.inner_own
  2.7 1.2 copy.28
  3.8 0.8 reshape.16.first_own
  4.6 1.3 %copy.24 = bf16[2,32,32,32]{3,2,1,0:T(8,128)(2,1)S(1)} copy(bf16[2,32,32,32]{2,3,0,1:T(8,128)(2,1)} %bitcast.25) | data formatting | bytes 262144 | tf_op jit(solution)/shard_map/transpose | solution.py:758
  5.9 1.2 reshape.18.outer_own
  7.1 44.7 %mix.1.mixed = bf16[128,16,256]{2,1,0:T(8,128)(2,1)} custom-call(bf16[20,128,1024]{2,1,0:T(8,128)(2,1)} %bitcast.21, bf16[256,1024]{1,0:T(8,128)(2,1)} %constant.36.clone.forward, bf16[256,128]{1,0:T(8,128)(2,1)} %reshape.16.first_own, bf16[32,768]{1,0:T(8,128)(2,1)} %reshape.17.inner_own, bf16[64,1024]{1,0:T(8,128)(2,1)} %reshape.18.outer_own, ...), custom_call_target="tpu_custom_call" | custom-call | tf_op jit(solution)/shard_map/mix/pallas_call | solution.py:428
  51.9 62.2 %finish.1 = bf16[20,128,1024]{2,1,0:T(8,128)(2,1)} custom-call(bf16[128,16,256]{2,1,0:T(8,128)(2,1)} %mix.1.mixed, bf16[8,256,256]{2,1,0:T(8,128)(2,1)} %constant.38.clone.back_far, bf16[20,128,1024]{2,1,0:T(8,128)(2,1)} %bitcast.22, bf16[256,1024]{1,0:T(8,128)(2,1)} %constant.37.clone.width, bf16[20,128]{1,0:T(8,128)(2,1)} %lift_weight.1, ...), custom_call_target="tpu_custom_call" | custom-call | tf_op jit(solution)/shard_map/finish/pallas_call | solution.py:674
  114.1 5.7 %copy.30 = bf16[1,20,128,1024]{3,2,1,0:T(8,128)(2,1)} copy(bf16[1,20,128,1024]{3,2,1,0:T(8,128)(2,1)} %bitcast.23) | data formatting | bytes 10485760
  (1 shorter events, 0.0 us)
Async XLA Ops:
  0.0 1.0 copy-start

commit v4 on v3

--- a/solution.py
+++ b/solution.py
@@ -173,10 +173,10 @@
 WAVES = 16
 SLOTS = 32
 EIGHT = 8
-CHUNKS = (64, 64)
-STARTS = (0, 64)
+CHUNKS = (32, 48, 48)
+STARTS = (0, 32, 80)
 LANES = 512
-ROWS = 256
+ROWS = 128
 PARTS = 2
 TURN = 8
 

time: 120 us -> 117 us (0.975)
  Pallas kernels: 107 us -> 104 us
    pallas_call x1, Pallas kernels: 62.2 us -> 59.2 us  [finish(): pl.pallas_call(finish_kernel, in_specs=[pl.BlockSpec(memory_space=pl.ANY...]
where the time goes in v4:
time: 117 us
  Pallas kernels  104 us (89%)
  local copies, waits for them, and re-layouts  11.1 us (9%)
    pallas_call x1, Pallas kernels, finish(): pl.pallas_call(finish_kernel, in_specs=[pl.BlockSpec(memory_space=pl.ANY...  59.2 us
    pallas_call x1, Pallas kernels, mix(): pl.pallas_call(mix_kernel, in_specs=[pl.BlockSpec(memory_space=pl.ANY if...  44.7 us
    unnamed x3, local copies, waits for them, and re-layouts  5.84 us

profile of v4, /device:TPU:0, one launch (start us, length us, event | category | flops | bytes accessed | tf_op | source)
XLA Modules:
  0.0 116.7 jit_solution(8847990726229044238)
XLA Ops:
  0.0 0.0 copy-start
  0.0 0.7 convert_bitcast_fusion
  0.7 0.1 pad.2.clone
  0.8 0.2 copy-done
  1.0 1.0 fusion
  1.9 0.8 reshape.17.inner_own
  2.7 1.2 copy.28
  3.8 0.8 reshape.16.first_own
  4.6 1.3 %copy.24 = bf16[2,32,32,32]{3,2,1,0:T(8,128)(2,1)S(1)} copy(bf16[2,32,32,32]{2,3,0,1:T(8,128)(2,1)} %bitcast.25) | data formatting | bytes 262144 | tf_op jit(solution)/shard_map/transpose | solution.py:758
  5.9 1.2 %reshape.18.outer_own = bf16[64,1024]{1,0:T(8,128)(2,1)} reshape(bf16[2,32,32,32]{3,2,1,0:T(8,128)(2,1)S(1)} %copy.24) | data formatting | bytes 262144 | tf_op jit(solution)/shard_map/reshape | solution.py:758
  7.1 44.7 %mix.1.mixed = bf16[128,16,256]{2,1,0:T(8,128)(2,1)} custom-call(bf16[20,128,1024]{2,1,0:T(8,128)(2,1)} %bitcast.21, bf16[256,1024]{1,0:T(8,128)(2,1)} %constant.36.clone.forward, bf16[256,128]{1,0:T(8,128)(2,1)} %reshape.16.first_own, bf16[32,768]{1,0:T(8,128)(2,1)} %reshape.17.inner_own, bf16[64,1024]{1,0:T(8,128)(2,1)} %reshape.18.outer_own, ...), custom_call_target="tpu_custom_call" | custom-call | tf_op jit(solution)/shard_map/mix/pallas_call | solution.py:428
  51.9 59.2 %finish.1 = bf16[20,128,1024]{2,1,0:T(8,128)(2,1)} custom-call(bf16[128,16,256]{2,1,0:T(8,128)(2,1)} %mix.1.mixed, bf16[8,256,256]{2,1,0:T(8,128)(2,1)} %constant.38.clone.back_far, bf16[20,128,1024]{2,1,0:T(8,128)(2,1)} %bitcast.22, bf16[256,1024]{1,0:T(8,128)(2,1)} %constant.37.clone.width, bf16[20,128]{1,0:T(8,128)(2,1)} %lift_weight.1, ...), custom_call_target="tpu_custom_call" | custom-call | tf_op jit(solution)/shard_map/finish/pallas_call | solution.py:674
  111.0 5.7 %copy.30 = bf16[1,20,128,1024]{3,2,1,0:T(8,128)(2,1)} copy(bf16[1,20,128,1024]{3,2,1,0:T(8,128)(2,1)} %bitcast.23) | data formatting | bytes 10485760
  (1 shorter events, 0.0 us)
Async XLA Ops:
  0.0 1.0 copy-start

commit v5 on v4

--- a/solution.py
+++ b/solution.py
@@ -186,8 +186,8 @@
 
 
 def mix_kernel(
-    fields_far, forward, first_own, inner_own, outer_own, height_far, place_far, bias_row, second, first_spread, spread,
-    mixed, fields, height, place, modes, arrived, first, inner, outer, stacked, placed, inner_wide, turned_inner, weights, rows,
+    fields_far, forward, first_core, inner_own, outer_own, height_far, place_far, bias_row, second, first_spread, spread,
+    mixed, first_wide, first_turned, first_own, fields, height, place, modes, arrived, first, inner, outer, stacked, placed, inner_wide, turned_inner, weights, rows,
     blocks, closing, carried, turned, load, send_plane, recv_plane, send_near, recv_near, send_modes, recv_modes,
 ):
     variables, row_count, points = fields.shape
@@ -263,6 +263,18 @@
             send_sem=send_modes.at[t - 1, c], recv_sem=recv_modes.at[t - 1, c],
             device_id=device, device_id_type=MESH,
         )
+
+    first_wide[...] = first_core[...].astype(jnp.float32)
+    along = lax.broadcasted_iota(jnp.int32, (rank, first_own.shape[1]), 1)
+    down = lax.broadcasted_iota(jnp.int32, (rank, first_own.shape[1]), 0)
+    joined = None
+    for k in range(packs // planes):
+        for a in range(rank):
+            first_turned[k, a * EIGHT:(a + 1) * EIGHT, :] = first_wide[k * EIGHT:(k + 1) * EIGHT, a, :]
+        here = jnp.where(along == down + k * rank, 1.0, 0.0).astype(jnp.bfloat16)
+        got = dense(first_turned[k].astype(jnp.bfloat16), here)
+        joined = got if joined is None else joined + got
+    first_own[...] = joined.astype(jnp.bfloat16)
 
     for n in range(3):
         for step in range(1, planes):
@@ -424,6 +436,7 @@
     wide = 4 * rank
     slots = inner.shape[1] // rank
     packs = kx2 // 2 // EIGHT
+    joined = (rank * EIGHT, first.shape[0] // EIGHT * rank)
     operands = (fields, forward, first, inner, outer, height, place, bias_row, second, first_spread, spread)
     return pl.pallas_call(
         mix_kernel,
@@ -431,12 +444,15 @@
         out_specs=pl.BlockSpec(memory_space=pltpu.VMEM),
         out_shape=jax.ShapeDtypeStruct((channels, waves, kx2), jnp.bfloat16),
         scratch_shapes=[
+            pltpu.VMEM(first.shape, jnp.float32),
+            pltpu.VMEM((first.shape[0] // EIGHT, rank * EIGHT, rank), jnp.float32),
+            pltpu.VMEM(joined, jnp.bfloat16),
             pltpu.VMEM(fields.shape, jnp.bfloat16),
             pltpu.VMEM(height.shape, jnp.bfloat16),
             pltpu.VMEM(place.shape, jnp.bfloat16),
             pltpu.VMEM((holders, 2 * waves, variables * row_count), jnp.bfloat16),
             pltpu.VMEM((holders, 2 * waves, variables * row_count), jnp.bfloat16),
-            pltpu.VMEM((planes,) + first.shape, jnp.bfloat16),
+            pltpu.VMEM((planes,) + joined, jnp.bfloat16),
             pltpu.VMEM((planes,) + inner.shape, jnp.bfloat16),
             pltpu.VMEM((planes,) + outer.shape, jnp.bfloat16),
             pltpu.VMEM((place.shape[1], depth), jnp.bfloat16),
@@ -464,8 +480,8 @@
     )(*operands)
 
 
-def gelu(h):
-    return h * (0.5 + 0.5 * lax.erf(h * (1.0 / math.sqrt(2.0))))
+def twice_gelu(h):
+    return h + h * lax.erf(h * (1.0 / math.sqrt(2.0)))
 
 
 def finish_kernel(
@@ -575,7 +591,7 @@
     chosen = dense(tall[:inner, :variables], out_weight[...]).astype(jnp.bfloat16)
     down = lax.broadcasted_iota(jnp.int32, (inner, channels * EIGHT), 0) % EIGHT
     along = lax.broadcasted_iota(jnp.int32, (inner, channels * EIGHT), 1) % EIGHT
-    closing[...] = jnp.where(down == along, dense(chosen, wide[...]), 0.0).astype(jnp.bfloat16)
+    closing[...] = jnp.where(down == along, 0.5 * dense(chosen, wide[...]), 0.0).astype(jnp.bfloat16)
     column = jnp.sum(tall[:inner, :variables].astype(jnp.float32) * out_bias[...], axis=1, keepdims=True)
     last_bias[...] = jnp.broadcast_to(column, last_bias.shape)
     relay_last(0)
@@ -616,7 +632,7 @@
                             dense(cols[x, part:part + ROWS, :], width[:, lanes])
                             + dense(skip[start + part:start + part + ROWS, :], source[x, :, lanes])
                         )
-                        active[lane * 2 + h, part:part + ROWS, :] = gelu(height).astype(jnp.bfloat16)
+                        active[lane * 2 + h, part:part + ROWS, :] = twice_gelu(height).astype(jnp.bfloat16)
                 for h in range(2):
                     x = 2 * i + h
                     got = dense(closing[:, start:start + size], active[lane * 2 + h, :size, :])
@@ -754,10 +770,9 @@
     lift = lax.dynamic_slice_in_dim(lift, lax.axis_index("batch") * count, count, 1)
     inner = jnp.einsum("vc,cde->dve", lift, input_core, preferred_element_type=jnp.float32)
     inner = inner.astype(jnp.bfloat16).reshape(rank, used * rank)
-    first = first_core.reshape(packs, EIGHT, rank, rank).transpose(2, 1, 0, 3).reshape(rank * EIGHT, packs * rank)
     outer = output_core.transpose(1, 0, 3, 2).reshape(2 * count, rank * rank)
     mixed = mix(
-        fields, forward, first, inner, outer, jnp.asarray(height), place, bias_row,
+        fields, forward, first_core, inner, outer, jnp.asarray(height), place, bias_row,
         second_core.reshape(waves * rank, rank), first_spread, spread, lax.axis_size("batch"),
     )
     return finish(

time: 117 us -> 115 us (0.983)
  local copies, waits for them, and re-layouts: 11.1 us -> 9.18 us
    reshape x2 -> x0, local copies, waits for them, and re-layouts: 1.95 us -> none  [fast_shards(): first_core.reshape(packs, EIGHT, rank, rank).transpose(2, 1, 0, 3)]
where the time goes in v5:
time: 115 us
  Pallas kernels  104 us (90%)
  local copies, waits for them, and re-layouts  9.18 us (8%)
    pallas_call x1, Pallas kernels, finish(): pl.pallas_call(finish_kernel, in_specs=[pl.BlockSpec(memory_space=pl.ANY...  58.7 us
    pallas_call x1, Pallas kernels, mix(): pl.pallas_call(mix_kernel, in_specs=[pl.BlockSpec(memory_space=pl.ANY if...  45.3 us
    unnamed x3, local copies, waits for them, and re-layouts  5.84 us

profile of v5, /device:TPU:0, one launch (start us, length us, event | category | flops | bytes accessed | tf_op | source)
XLA Modules:
  0.0 114.9 jit_solution(9658471484646544334)
XLA Ops:
  0.0 0.0 copy-start
  0.0 0.7 convert_bitcast_fusion
  0.7 0.1 pad.2.clone
  0.8 0.2 copy-done
  1.0 1.0 fusion
  1.9 0.8 reshape.9.inner_own
  2.7 1.3 %copy.23 = bf16[2,32,32,32]{3,2,1,0:T(8,128)(2,1)S(1)} copy(bf16[2,32,32,32]{2,3,0,1:T(8,128)(2,1)} %bitcast.20) | data formatting | bytes 262144 | tf_op jit(solution)/shard_map/transpose | solution.py:773
  4.0 1.2 %reshape.10.outer_own = bf16[64,1024]{1,0:T(8,128)(2,1)} reshape(bf16[2,32,32,32]{3,2,1,0:T(8,128)(2,1)S(1)} %copy.23) | data formatting | bytes 262144 | tf_op jit(solution)/shard_map/reshape | solution.py:773
  5.2 45.3 %mix.1.mixed = bf16[128,16,256]{2,1,0:T(8,128)(2,1)} custom-call(bf16[20,128,1024]{2,1,0:T(8,128)(2,1)} %bitcast.17, bf16[256,1024]{1,0:T(8,128)(2,1)} %constant.36.clone.forward, bf16[32,32,32]{2,1,0:T(8,128)(2,1)} %first_core.1, bf16[32,768]{1,0:T(8,128)(2,1)} %reshape.9.inner_own, bf16[64,1024]{1,0:T(8,128)(2,1)} %reshape.10.outer_own, ...), custom_call_target="tpu_custom_call" | custom-call | tf_op jit(solution)/shard_map/mix/pallas_call | solution.py:441
  50.5 58.7 %finish.1 = bf16[20,128,1024]{2,1,0:T(8,128)(2,1)} custom-call(bf16[128,16,256]{2,1,0:T(8,128)(2,1)} %mix.1.mixed, bf16[8,256,256]{2,1,0:T(8,128)(2,1)} %constant.38.clone.back_far, bf16[20,128,1024]{2,1,0:T(8,128)(2,1)} %bitcast.18, bf16[256,1024]{1,0:T(8,128)(2,1)} %constant.37.clone.width, bf16[20,128]{1,0:T(8,128)(2,1)} %lift_weight.1, ...), custom_call_target="tpu_custom_call" | custom-call | tf_op jit(solution)/shard_map/finish/pallas_call | solution.py:690
  109.3 5.7 %copy.27 = bf16[1,20,128,1024]{3,2,1,0:T(8,128)(2,1)} copy(bf16[1,20,128,1024]{3,2,1,0:T(8,128)(2,1)} %bitcast.19) | data formatting | bytes 10485760
  (1 shorter events, 0.0 us)
Async XLA Ops:
  0.0 1.0 copy-start

commit v6 on v5

--- a/solution.py
+++ b/solution.py
@@ -178,7 +178,7 @@
 LANES = 512
 ROWS = 128
 PARTS = 2
-TURN = 8
+TURN = 16
 
 
 def whole(a):

time: 115 us -> 114 us (level)
  no operation moved by 1% of the time
where the time goes in v6:
time: 114 us
  Pallas kernels  103 us (90%)
  local copies, waits for them, and re-layouts  9.18 us (8%)
    pallas_call x1, Pallas kernels, finish(): pl.pallas_call(finish_kernel, in_specs=[pl.BlockSpec(memory_space=pl.ANY...  58 us
    pallas_call x1, Pallas kernels, mix(): pl.pallas_call(mix_kernel, in_specs=[pl.BlockSpec(memory_space=pl.ANY if...  45.3 us
    unnamed x3, local copies, waits for them, and re-layouts  5.84 us

profile of v6, /device:TPU:0, one launch (start us, length us, event | category | flops | bytes accessed | tf_op | source)
XLA Modules:
  0.0 114.2 jit_solution(585344430208164799)
XLA Ops:
  0.0 0.0 copy-start
  0.0 0.7 convert_bitcast_fusion
  0.7 0.1 pad.2.clone
  0.8 0.2 copy-done
  1.0 1.0 fusion
  1.9 0.8 reshape.9.inner_own
  2.7 1.3 %copy.23 = bf16[2,32,32,32]{3,2,1,0:T(8,128)(2,1)S(1)} copy(bf16[2,32,32,32]{2,3,0,1:T(8,128)(2,1)} %bitcast.20) | data formatting | bytes 262144 | tf_op jit(solution)/shard_map/transpose | solution.py:773
  4.0 1.2 %reshape.10.outer_own = bf16[64,1024]{1,0:T(8,128)(2,1)} reshape(bf16[2,32,32,32]{3,2,1,0:T(8,128)(2,1)S(1)} %copy.23) | data formatting | bytes 262144 | tf_op jit(solution)/shard_map/reshape | solution.py:773
  5.2 45.3 %mix.1.mixed = bf16[128,16,256]{2,1,0:T(8,128)(2,1)} custom-call(bf16[20,128,1024]{2,1,0:T(8,128)(2,1)} %bitcast.17, bf16[256,1024]{1,0:T(8,128)(2,1)} %constant.36.clone.forward, bf16[32,32,32]{2,1,0:T(8,128)(2,1)} %first_core.1, bf16[32,768]{1,0:T(8,128)(2,1)} %reshape.9.inner_own, bf16[64,1024]{1,0:T(8,128)(2,1)} %reshape.10.outer_own, ...), custom_call_target="tpu_custom_call" | custom-call | tf_op jit(solution)/shard_map/mix/pallas_call | solution.py:441
  50.5 58.0 %finish.1 = bf16[20,128,1024]{2,1,0:T(8,128)(2,1)} custom-call(bf16[128,16,256]{2,1,0:T(8,128)(2,1)} %mix.1.mixed, bf16[8,256,256]{2,1,0:T(8,128)(2,1)} %constant.38.clone.back_far, bf16[20,128,1024]{2,1,0:T(8,128)(2,1)} %bitcast.18, bf16[256,1024]{1,0:T(8,128)(2,1)} %constant.37.clone.width, bf16[20,128]{1,0:T(8,128)(2,1)} %lift_weight.1, ...), custom_call_target="tpu_custom_call" | custom-call | tf_op jit(solution)/shard_map/finish/pallas_call | solution.py:690
  108.5 5.7 %copy.27 = bf16[1,20,128,1024]{3,2,1,0:T(8,128)(2,1)} copy(bf16[1,20,128,1024]{3,2,1,0:T(8,128)(2,1)} %bitcast.19) | data formatting | bytes 10485760
  (1 shorter events, 0.0 us)
Async XLA Ops:
  0.0 1.0 copy-start

commit v7 on v6

--- a/solution.py
+++ b/solution.py
@@ -335,11 +335,11 @@
                     ).astype(jnp.bfloat16)
         return carry
 
-    lax.fori_loop(0, pairs, weight_step, 0)
-
+    lax.fori_loop(0, pairs // 2, weight_step, 0)
     for step in range(1, planes):
         plane_copy(step, 2).wait_recv()
         near_copy(step, 2).start()
+    lax.fori_loop(pairs // 2, pairs, weight_step, 0)
     for step in range(1, planes):
         near_copy(step, 2).wait_recv()
     count = channels // planes

time: 114 us -> 114 us (level)
    pallas_call x1, Pallas kernels: 45.3 us -> 43.2 us  [mix(): pl.pallas_call(mix_kernel, in_specs=[pl.BlockSpec(memory_space=pl.ANY if...]
    pallas_call x1, Pallas kernels: 58 us -> 60 us  [finish(): pl.pallas_call(finish_kernel, in_specs=[pl.BlockSpec(memory_space=pl.ANY...]
where the time goes in v7:
time: 114 us
  Pallas kernels  103 us (90%)
  local copies, waits for them, and re-layouts  9.18 us (8%)
    pallas_call x1, Pallas kernels, finish(): pl.pallas_call(finish_kernel, in_specs=[pl.BlockSpec(memory_space=pl.ANY...  60 us
    pallas_call x1, Pallas kernels, mix(): pl.pallas_call(mix_kernel, in_specs=[pl.BlockSpec(memory_space=pl.ANY if...  43.2 us
    unnamed x3, local copies, waits for them, and re-layouts  5.84 us

profile of v7, /device:TPU:0, one launch (start us, length us, event | category | flops | bytes accessed | tf_op | source)
XLA Modules:
  0.0 114.1 jit_solution(5252317641907567198)
XLA Ops:
  0.0 0.0 copy-start
  0.0 0.7 convert_bitcast_fusion
  0.7 0.1 pad.2.clone
  0.8 0.2 copy-done
  1.0 1.0 fusion
  1.9 0.8 reshape.9.inner_own
  2.7 1.3 %copy.23 = bf16[2,32,32,32]{3,2,1,0:T(8,128)(2,1)S(1)} copy(bf16[2,32,32,32]{2,3,0,1:T(8,128)(2,1)} %bitcast.20) | data formatting | bytes 262144 | tf_op jit(solution)/shard_map/transpose | solution.py:773
  4.0 1.2 %reshape.10.outer_own = bf16[64,1024]{1,0:T(8,128)(2,1)} reshape(bf16[2,32,32,32]{3,2,1,0:T(8,128)(2,1)S(1)} %copy.23) | data formatting | bytes 262144 | tf_op jit(solution)/shard_map/reshape | solution.py:773
  5.2 43.2 %mix.1.mixed = bf16[128,16,256]{2,1,0:T(8,128)(2,1)} custom-call(bf16[20,128,1024]{2,1,0:T(8,128)(2,1)} %bitcast.17, bf16[256,1024]{1,0:T(8,128)(2,1)} %constant.36.clone.forward, bf16[32,32,32]{2,1,0:T(8,128)(2,1)} %first_core.1, bf16[32,768]{1,0:T(8,128)(2,1)} %reshape.9.inner_own, bf16[64,1024]{1,0:T(8,128)(2,1)} %reshape.10.outer_own, ...), custom_call_target="tpu_custom_call" | custom-call | tf_op jit(solution)/shard_map/mix/pallas_call | solution.py:441
  48.4 60.0 %finish.1 = bf16[20,128,1024]{2,1,0:T(8,128)(2,1)} custom-call(bf16[128,16,256]{2,1,0:T(8,128)(2,1)} %mix.1.mixed, bf16[8,256,256]{2,1,0:T(8,128)(2,1)} %constant.38.clone.back_far, bf16[20,128,1024]{2,1,0:T(8,128)(2,1)} %bitcast.18, bf16[256,1024]{1,0:T(8,128)(2,1)} %constant.37.clone.width, bf16[20,128]{1,0:T(8,128)(2,1)} %lift_weight.1, ...), custom_call_target="tpu_custom_call" | custom-call | tf_op jit(solution)/shard_map/finish/pallas_call | solution.py:690
  108.5 5.7 %copy.27 = bf16[1,20,128,1024]{3,2,1,0:T(8,128)(2,1)} copy(bf16[1,20,128,1024]{3,2,1,0:T(8,128)(2,1)} %bitcast.19) | data formatting | bytes 10485760
  (1 shorter events, 0.0 us)
Async XLA Ops:
  0.0 1.0 copy-start
